TPU v7x, 32 devices: a whole 2x2x4 slice. The times are simulated.
32 devices in a mesh: leaf: 4 (over z), grid: 8 (over y, x, core).
Axes of the slice: x: 2, y: 2, z: 4, core: 2. Of those that a mesh axis runs over, the one named last changes fastest.
Arguments:
- root_inverse: float32 [4096, 4096], P('grid', 'leaf'), may hold values from -1 to 12, as said below
- middle_inverse: float32 [2048, 4096], P('grid', 'leaf'), may hold values from -1 to 12, as said below
- middle_panel: float32 [4096, 4096], P('grid', 'leaf'), may hold values from -0.1875 to 0.1875
- lower_root: float32 [4096, 8192], P('grid', 'leaf'), may hold values from -0.1875 to 0.1875
- lower_middle: float32 [2048, 8192], P(None, 'leaf'), may hold values from -0.25 to 0.25
- block_pattern: int32 [4, 32], replicated, may hold values 0 or 1
- lower_diagonal: float32 [8192], P('leaf'), may hold values from 1.5 to 6
Outputs:
- middle_cross: float32 [4096, 4096], P('grid', 'leaf')
- middle_variance: float32 [4096], P('leaf')
- lower_cross: float32 [4096, 8192], P('grid', 'leaf')
- lower_parent: float32 [2048, 8192], P('grid', 'leaf')
- lower_variance: float32 [8192], P('leaf')
Inputs may be any that keep to these rules, and one draw needn't show every extreme that they name: `root_inverse`: symmetric; its diagonal entries lie between 1.5 and 12. `middle_inverse`: each front's 2048 x 2048 block is symmetric; its diagonal entries lie between 1.5 and 12.
All inputs are finite; a program needn't handle non-finite values.
Results may differ from a plain program's by a relative error of at most 0.0001.
Values sent between devices are 32-bit elements; how exact they have to be, the bound alone decides.
No kernel may reach another device: no remote copies, remote signals or barrier semaphores. Data moves between devices by JAX's collectives and lax.ppermute only.
A program may use at most 192 MiB of HBM per device.

v0:
```python
import jax
import jax.numpy as jnp
from jax import lax
from jax.sharding import PartitionSpec as P

S1 = 2048
BLK = 128


exact = lax.Precision.HIGHEST


def root_times(panel, root_rows):
    return lax.psum_scatter(
        lax.dot_general(
            root_rows,
            panel,
            (((0,), (0,)), ((), ())),
            precision=exact,
            preferred_element_type=jnp.float32,
        ),
        "grid",
        scatter_dimension=0,
        tiled=True,
    )


def local(
    root_inverse,
    middle_inverse,
    middle_panel,
    lower_root,
    lower_middle,
    block_pattern,
    lower_diagonal,
):
    leaf_count = lax.axis_size("leaf")
    leaf_index = lax.axis_index("leaf")
    grid_index = lax.axis_index("grid")
    parent_front = leaf_index // (leaf_count // 2)
    child_front = leaf_index // (leaf_count // 4)
    root_rows, middle_rows, middle_block = (
        lax.all_gather(root_inverse, "leaf", axis=1, tiled=True),
        lax.all_gather(middle_panel, "leaf", axis=1, tiled=True),
        lax.all_gather(middle_inverse, "leaf", axis=1, tiled=True),
    )
    middle_rows = lax.dynamic_slice_in_dim(middle_rows, parent_front * S1, S1, 1)
    middle_block = lax.dynamic_slice_in_dim(middle_block, parent_front * S1, S1, 1)
    local_rows = lower_root.shape[0]
    blocks_here = local_rows // BLK
    pattern = lax.dynamic_slice(
        block_pattern, (child_front, grid_index * blocks_here), (1, blocks_here)
    )
    keep = jnp.repeat(pattern[0].astype(jnp.float32), BLK)
    lower_panel = lower_root * keep[:, None]
    first_side = root_times(middle_panel, root_rows)
    reduced = lower_panel - jnp.dot(
        middle_rows, lower_middle, precision=exact, preferred_element_type=jnp.float32
    )
    root_side = root_times(reduced, root_rows)
    parent_own = jnp.dot(
        middle_block, lower_middle, precision=exact, preferred_element_type=jnp.float32
    )
    middle_count = middle_inverse.shape[0]
    parent_side = parent_own - lax.psum_scatter(
        lax.dot_general(
            middle_rows,
            root_side,
            (((0,), (0,)), ((), ())),
            precision=exact,
            preferred_element_type=jnp.float32,
        ),
        "grid",
        scatter_dimension=0,
        tiled=True,
    )
    own_columns = middle_inverse.shape[1]
    global_rows = grid_index * middle_count + jnp.arange(middle_count, dtype=jnp.int32)
    global_columns = leaf_index % (leaf_count // 2) * own_columns + jnp.arange(
        own_columns, dtype=jnp.int32
    )
    on_diagonal = global_rows[:, None] == global_columns[None, :]
    middle_part = jnp.sum(jnp.where(on_diagonal, middle_inverse, 0.0), axis=0) + jnp.sum(
        middle_panel * first_side, axis=0
    )
    lower_rows = lax.dynamic_slice_in_dim(lower_middle, grid_index * middle_count, middle_count, 0)
    lower_part = jnp.sum(lower_panel * root_side, axis=0) + jnp.sum(
        lower_rows * parent_side, axis=0
    )
    middle_total, lower_total = lax.psum((middle_part, lower_part), "grid")
    return (-first_side, middle_total, -root_side, -parent_side, lower_diagonal + lower_total)


def solution(mesh):
    in_specs = (
        P("grid", "leaf"),
        P("grid", "leaf"),
        P("grid", "leaf"),
        P("grid", "leaf"),
        P(None, "leaf"),
        P(),
        P("leaf"),
    )
    out_specs = (P("grid", "leaf"), P("leaf"), P("grid", "leaf"), P("grid", "leaf"), P("leaf"))
    return jax.shard_map(local, mesh=mesh, in_specs=in_specs, out_specs=out_specs, check_vma=False)
```

profile of v0, /device:TPU:0, one launch (start us, length us, event | category | flops | bytes accessed | tf_op | source)
XLA Modules:
  0.0 947.9 jit_solution(12877820143338143006)
XLA Ops:
  7.2 0.0 all-gather.6.cloned.1.call-start
  7.2 0.7 all-gather.6.cloned.1.call-update
  7.9 0.0 all-gather.4.cloned.1.call-start
  7.9 0.7 all-gather.4.cloned.1.call-update
  8.6 0.0 reduce-scatter.6.cloned.1.call-start
  8.7 5.4 copy.12
  14.1 0.8 convert_bitcast_fusion
  14.8 0.1 broadcast_bitcast_fusion
  14.9 147.0 %all-gather.6.cloned.1.call-done = f32[512,4096]{1,0:T(8,128)} async-done(((f32[512,1024]{1,0:T(8,128)}), f32[512,4096]{1,0:T(8,128)}) %all-gather.6.cloned.1.call-update) | async-done | bytes 8388624 | tf_op jit(solution)/shard_map/all_gather | solution.py:44
  161.9 31.6 %fusion.4 = f32[512,2048]{0,1:T(8,128)} fusion(f32[2048,2048]{1,0:T(8,128)} %param.11, f32[512,4096]{1,0:T(8,128)} %all-gather.6.cloned.1.call-done, s32[]{:T(128)S(6)} %select_n.34), kind=kOutput, calls=%fused_computation.6 | convolution fusion | flops 25769803776 | bytes 25165828 | tf_op jit(solution)/shard_map/dot_general | solution.py:57
  193.6 117.8 %all-gather.4.cloned.1.call-done = f32[512,4096]{1,0:T(8,128)} async-done(((f32[512,1024]{1,0:T(8,128)}), f32[512,4096]{1,0:T(8,128)}) %all-gather.4.cloned.1.call-update) | async-done | bytes 8388624 | tf_op jit(solution)/shard_map/all_gather | solution.py:43
  311.4 60.9 %convolution_bitcast_fusion = f32[4096,2048]{0,1:T(8,128)} fusion(f32[512,4096]{1,0:T(8,128)} %all-gather.4.cloned.1.call-done, f32[512,2048]{0,1:T(8,128)} %fusion.4, f32[512,2048]{0,1:T(8,128)} %copy.12, f32[512]{0:T(512)S(1)} %broadcast_bitcast_fusion), kind=kOutput, calls=%fused_computation | convolution fusion | flops 51541704704 | bytes 50333696 | tf_op jit(solution)/shard_map/dot_general | solution.py:15
  372.3 0.0 copy-start.1
  372.3 0.0 reduce-scatter.6.cloned.1.call-update
  372.4 0.0 reduce-scatter.4.cloned.1.call-start
  372.4 1.5 copy-done.1
  373.9 31.0 %fusion.13 = f32[4096,1024]{1,0:T(8,128)} fusion(f32[512,4096]{1,0:T(8,128)} %all-gather.4.cloned.1.call-done, f32[512,1024]{1,0:T(8,128)S(1)} %copy-done.1), kind=kOutput, calls=%fused_computation.23 | convolution fusion | flops 25769803776 | bytes 27262976 | tf_op jit(solution)/shard_map/dot_general | solution.py:15
  404.9 0.0 reduce-scatter.4.cloned.1.call-update
  404.9 0.0 all-gather.8.cloned.1.call-start
  405.0 0.5 all-gather.8.cloned.1.call-update
  405.5 0.0 reduce-scatter.8.cloned.1.call-start
  405.5 170.4 %reduce-scatter.6.cloned.1.call-done = f32[512,2048]{0,1:T(8,128)} async-done(((f32[4096,2048]{0,1:T(8,128)}), f32[512,2048]{0,1:T(8,128)}) %reduce-scatter.6.cloned.1.call-update) | async-done | bytes 4194320 | tf_op jit(solution)/shard_map/reduce_scatter | solution.py:14
  575.9 57.4 %fusion.2 = f32[2048,2048]{1,0:T(8,128)} fusion(f32[512,2048]{0,1:T(8,128)} %reduce-scatter.6.cloned.1.call-done, f32[512,4096]{1,0:T(8,128)} %all-gather.6.cloned.1.call-done, s32[]{:T(128)S(6)} %select_n.34), kind=kOutput, calls=%fused_computation.4 | convolution fusion | flops 25769803776 | bytes 25165828 | tf_op jit(solution)/shard_map/dot_general | solution.py:66
  633.4 0.0 copy-start.2
  633.4 0.0 reduce-scatter.8.cloned.1.call-update
  633.5 1.2 copy-done.2
  634.7 0.2 select_reduce_fusion
  634.9 60.9 %reduce-scatter.4.cloned.1.call-done = f32[512,1024]{1,0:T(8,128)} async-done(((f32[4096,1024]{1,0:T(8,128)}), f32[512,1024]{1,0:T(8,128)}) %reduce-scatter.4.cloned.1.call-update) | async-done | bytes 2097168 | tf_op jit(solution)/shard_map/reduce_scatter | solution.py:14
  695.8 0.0 copy-start
  695.8 3.5 multiply_reduce_fusion.2
  699.3 0.0 copy-done
  699.3 4.7 fusion.11
  704.0 5.6 copy.13
  709.7 0.0 copy-start.3
  709.7 68.4 %all-gather.8.cloned.1.call-done = f32[256,4096]{1,0:T(8,128)} async-done(((f32[256,1024]{1,0:T(8,128)}), f32[256,4096]{1,0:T(8,128)}) %all-gather.8.cloned.1.call-update) | async-done | bytes 4194320 | tf_op jit(solution)/shard_map/all_gather | solution.py:45
  778.1 118.4 %reduce-scatter.8.cloned.1.call-done = f32[256,2048]{1,0:T(8,128)} async-done(((f32[2048,2048]{1,0:T(8,128)}), f32[256,2048]{1,0:T(8,128)}) %reduce-scatter.8.cloned.1.call-update) | async-done | bytes 2097168 | tf_op jit(solution)/shard_map/reduce_scatter | solution.py:65
  896.4 20.6 %fusion.12 = (f32[256,2048]{1,0:T(8,128)}, f32[2048]{0:T(1024)S(1)}) fusion(f32[2048,2048]{1,0:T(8,128)} %param.11, s32[]{:T(128)S(6)} %select_n.35, f32[256,2048]{1,0:T(8,128)} %reduce-scatter.8.cloned.1.call-done, f32[256,4096]{1,0:T(8,128)} %all-gather.8.cloned.1.call-done, s32[]{:T(128)S(6)} %select_n.34), kind=kOutput, calls=%fused_computation.22 | convolution fusion | flops 12886996992 | bytes 25174024 | tf_op jit(solution)/shard_map/dot_general | solution.py:61
  917.0 23.0 %all-reduce = (f32[1024]{0:T(1024)}, f32[2048]{0:T(1024)S(1)}) all-reduce(f32[1024]{0:T(1024)S(1)} %add.63, f32[2048]{0:T(1024)S(1)} %add.68), channel_id=1, replica_groups=mesh['leaf'=4,'grid'=8] {'grid'}, use_global_device_ids=true, to_apply=%region_3.4 | all-reduce | flops 3072 | bytes 24576 | tf_op jit(solution)/shard_map/psum | solution.py:90
  940.0 0.0 copy-done.3
  940.0 0.6 add.69
  (4 shorter events, 0.0 us)
Async XLA Ops:
  7.2 154.8 %all-gather.6.cloned.1.call-start = ((), (), s32[]{:S(2)}) async-start(), calls=%async_computation.5 | async-start | bytes 10485760 | tf_op jit(solution)/shard_map/all_gather | solution.py:44
  7.9 303.5 %all-gather.4.cloned.1.call-start = ((), (), s32[]{:S(2)}) async-start(), calls=%async_computation.3 | async-start | bytes 10485760 | tf_op jit(solution)/shard_map/all_gather | solution.py:43
  8.6 567.3 %reduce-scatter.6.cloned.1.call-start = ((), (), s32[]{:S(2)}) async-start(), calls=%async_computation.6 | async-start | bytes 37748736 | tf_op jit(solution)/shard_map/reduce_scatter | solution.py:14
  372.3 1.6 copy-start.1
  372.4 323.4 %reduce-scatter.4.cloned.1.call-start = ((), (), s32[]{:S(2)}) async-start(), calls=%async_computation.4 | async-start | bytes 18874368 | tf_op jit(solution)/shard_map/reduce_scatter | solution.py:14
  404.9 373.2 %all-gather.8.cloned.1.call-start = ((), (), s32[]{:S(2)}) async-start(), calls=%async_computation.7 | async-start | bytes 5242880 | tf_op jit(solution)/shard_map/all_gather | solution.py:45
  405.5 490.9 %reduce-scatter.8.cloned.1.call-start = ((), (), s32[]{:S(2)}) async-start(), calls=%async_computation.8 | async-start | bytes 18874368 | tf_op jit(solution)/shard_map/reduce_scatter | solution.py:65
  633.4 1.3 copy-start.2
  695.8 3.5 copy-start
  709.7 230.4 %copy-start.3 = (f32[2048]{0:T(1024)S(1)}, f32[2048]{0:T(1024)}, u32[]{:S(2)}) copy-start(f32[2048]{0:T(1024)} %param.13) | copy-start | bytes 24580
Sparse Core Ops, SparseCore 0:
  9.6 152.3 all-gather.5
  163.5 147.8 all-gather.3
  372.5 203.4 reduce-scatter.5
  579.8 115.9 reduce-scatter.3
  697.3 80.7 all-gather.7
  781.9 114.4 reduce-scatter.7
where the time goes:
time: 954 us; the launch traced here: 948 us
  waiting for transfers between devices  685 us (72%)
  matrix products  202 us (21%)
  blocking collectives  23 us (2%)
  between operations  14.6 us (2%)
  local copies, waits for them, and re-layouts  13.8 us (1%)
  other arithmetic  9.82 us (1%)
    reduce_scatter x2, waiting for transfers between devices, root_times(): lax.psum_scatter(lax.dot_general(root_rows, panel, (((0,), (0,)), ((), ()...  231 us
    all_gather x1, waiting for transfers between devices, local(): lax.all_gather(middle_panel, 'leaf', axis=1, tiled=True)  147 us
    reduce_scatter x1, waiting for transfers between devices, local(): lax.psum_scatter(lax.dot_general(middle_rows, root_side, (((0,), (0,)), (...  118 us
    all_gather x1, waiting for transfers between devices, local(): lax.all_gather(root_inverse, 'leaf', axis=1, tiled=True)  118 us
    dot_general x2, matrix products, root_times(): lax.dot_general(root_rows, panel, (((0,), (0,)), ((), ())), precision=exa...  91.9 us
    all_gather x1, waiting for transfers between devices, local(): lax.all_gather(middle_inverse, 'leaf', axis=1, tiled=True)  68.4 us
    dot_general x1, matrix products, local(): lax.dot_general(middle_rows, root_side, (((0,), (0,)), ((), ())), precisi...  57.4 us
    dot_general x1, matrix products, local(): jnp.dot(middle_rows, lower_middle, precision=exact, preferred_element_typ...  31.6 us
  transfers between devices with their start and end apart: 6, of which 6 were waited for; matrix products, arithmetic and copies ran while one was open for 15% of the time, Pallas kernels for 0%

commit v1 on v0

v1 whole, which is shorter than its diff:
```python
import functools

import jax
import jax.numpy as jnp
from jax import lax
from jax.experimental import pallas as pl
from jax.experimental.pallas import tpu as pltpu
from jax.sharding import PartitionSpec as P

BLK = 128


near = lax.Precision.HIGH


def dot(left, right):
    return lax.dot_general(
        left, right, (((1,), (0,)), ((), ())), precision=near, preferred_element_type=jnp.float32
    )


def split(value):
    high = value.astype(jnp.bfloat16)
    return high, (value - high.astype(jnp.float32)).astype(jnp.bfloat16)


def split_dot(left_high, left_low, right_high, right_low):
    def one(left, right):
        return jnp.dot(left, right, preferred_element_type=jnp.float32)

    return one(left_high, right_high) + (one(left_high, right_low) + one(left_low, right_high))


def split_blocks(block_refs, high_ref, low_ref):
    start = 0
    for block_ref in block_refs:
        place = slice(start, start + block_ref.shape[0])
        high_ref[place, :], low_ref[place, :] = split(block_ref[...])
        start += block_ref.shape[0]


def root_kernel(count, index_ref, root_ref, *refs):
    block_refs, out_ref = refs[:-5], refs[-5]
    root_high, root_low, high, low = refs[-4:]
    rows = root_ref.shape[1] // count

    @pl.when(pl.program_id(0) == 0)
    def _():
        for e in range(count):
            place = slice(e * rows, (e + 1) * rows)
            start = pl.multiple_of((index_ref[0] ^ e) * rows, rows)
            root_high[:, place], root_low[:, place] = split(root_ref[:, pl.ds(start, rows)])

    split_blocks(block_refs, high, low)
    out_ref[...] = split_dot(root_high[...], root_low[...], high[...], low[...])


def side_kernel(count, *refs):
    column_refs, block_refs, out_ref = refs[:count], refs[count:-5], refs[-5]
    side_high, side_low, high, low = refs[-4:]

    @pl.when(pl.program_id(0) == 0)
    def _():
        start = 0
        for column_ref in column_refs:
            place = slice(start, start + column_ref.shape[0])
            start += column_ref.shape[0]
            side_high[:, place], side_low[:, place] = split(column_ref[...].T)

    split_blocks(block_refs, high, low)
    out_ref[...] = split_dot(side_high[...], side_low[...], high[...], low[...])


def panel_scratch(height, depth, tile):
    return [
        pltpu.VMEM((height, depth), jnp.bfloat16),
        pltpu.VMEM((height, depth), jnp.bfloat16),
        pltpu.VMEM((depth, tile), jnp.bfloat16),
        pltpu.VMEM((depth, tile), jnp.bfloat16),
    ]


def panel_cost(height, depth, width):
    return pl.CostEstimate(
        flops=6 * height * depth * width,
        transcendentals=0,
        bytes_accessed=4 * (height * depth + depth * width + height * width),
    )


def whole_spec(array, index):
    return pl.BlockSpec(array.shape, index, pipeline_mode=pl.Buffered(1))


def root_times(index, root_rows, blocks, row=0, rows=1):
    height, depth = root_rows.shape[0] // rows, root_rows.shape[1]
    count = lax.axis_size("grid")
    width = blocks[0].shape[1]
    tile = min(width, 256)
    return pl.pallas_call(
        functools.partial(root_kernel, count),
        grid_spec=pltpu.PrefetchScalarGridSpec(
            num_scalar_prefetch=1,
            grid=(width // tile,),
            in_specs=[
                pl.BlockSpec(
                    (height, depth), lambda i, s: (row, 0), pipeline_mode=pl.Buffered(1)
                )
            ]
            + [pl.BlockSpec((block.shape[0], tile), lambda i, s: (0, i)) for block in blocks],
            out_specs=pl.BlockSpec((height, tile), lambda i, s: (0, i)),
            scratch_shapes=panel_scratch(height, depth, tile),
        ),
        out_shape=jax.ShapeDtypeStruct((height, width), jnp.float32),
        compiler_params=pltpu.CompilerParams(vmem_limit_bytes=44 * 2**20),
        cost_estimate=panel_cost(height, depth, width),
    )(index, root_rows, *blocks)


def side_times(columns, blocks):
    height = columns[0].shape[1]
    depth = sum(block.shape[0] for block in blocks)
    width = blocks[0].shape[1]
    tile = min(width, 256)
    return pl.pallas_call(
        functools.partial(side_kernel, len(columns)),
        grid=(width // tile,),
        in_specs=[whole_spec(column, lambda i: (0, 0)) for column in columns]
        + [pl.BlockSpec((block.shape[0], tile), lambda i: (0, i)) for block in blocks],
        out_specs=pl.BlockSpec((height, tile), lambda i: (0, i)),
        scratch_shapes=panel_scratch(height, depth, tile),
        out_shape=jax.ShapeDtypeStruct((height, width), jnp.float32),
        compiler_params=pltpu.CompilerParams(vmem_limit_bytes=44 * 2**20),
        cost_estimate=panel_cost(height, depth, width),
    )(*columns, *blocks)


def after(value, other):
    return lax.optimization_barrier((value, other))[0]


def swap(value, axis, flip):
    count = lax.axis_size(axis)
    return lax.ppermute(value, axis, [(i, i ^ flip) for i in range(count)])


def gather_chips(own, before=()):
    half = own.shape[0] // 2
    across, along, core = swap(own, "grid", 2), swap(own, "grid", 4), swap(own, "grid", 1)
    held = after([across, along], (core, before))
    onward = [held[0][:half], held[1][half:]]
    diagonal = [swap(onward[0], "grid", 4), swap(onward[1], "grid", 2)]
    blocks = {0: [own], 1: [core], 2: [across], 4: [along], 6: diagonal}
    blocks[3], blocks[5] = [swap(across, "grid", 1)], [swap(along, "grid", 1)]
    return blocks, onward


def doubled_hops(own):
    blocks, flip = {0: [own]}, 2
    while flip < lax.axis_size("grid"):
        for e in list(blocks):
            blocks[e | flip] = [swap(part, "grid", flip) for part in blocks[e]]
        flip *= 2
    return blocks


def gather_cores(blocks):
    for e in list(blocks):
        if e | 1 not in blocks:
            blocks[e | 1] = [swap(part, "grid", 1) for part in blocks[e]]
    return [part for e in range(len(blocks)) for part in blocks[e]]


def local(
    root_inverse,
    middle_inverse,
    middle_panel,
    lower_root,
    lower_middle,
    block_pattern,
    lower_diagonal,
):
    leaf_count = lax.axis_size("leaf")
    grid_count = lax.axis_size("grid")
    leaf_index = lax.axis_index("leaf")
    grid_index = lax.axis_index("grid")
    siblings = leaf_count // 2
    sibling_index = leaf_index % siblings
    child_front = leaf_index // (leaf_count // 4)
    local_rows = lower_root.shape[0]
    own_columns = middle_inverse.shape[1]
    middle_count = middle_inverse.shape[0]

    square = grid_count == 8
    index = grid_index.astype(jnp.int32).reshape((1,))
    width = lower_root.shape[1]
    chunk = min(width, 1024)
    chunks = range(width // chunk)

    def middle_rows(s):
        return lax.dynamic_slice_in_dim(
            lower_middle, (sibling_index ^ s) * own_columns, own_columns, 0
        )

    blocks_here = local_rows // BLK
    pattern = lax.dynamic_slice(
        block_pattern, (child_front, grid_index * blocks_here), (1, blocks_here)
    )
    keep = jnp.repeat(pattern[0].astype(jnp.float32), BLK)
    lower_panel = lower_root * keep[:, None]
    root_rows = lax.all_gather(root_inverse, "leaf", axis=1, tiled=True)
    panels = [lower_panel[:, c * chunk : (c + 1) * chunk] for c in chunks]
    if square:
        middle_blocks, _ = gather_chips(middle_panel)
        first_blocks, _ = gather_chips(panels[0])
        near_by = [first_blocks[e] for e in (3, 5)]
    else:
        middle_blocks = doubled_hops(middle_panel)
        first_blocks, near_by = doubled_hops(panels[0]), []
    middle_blocks = gather_cores(middle_blocks)
    lower_blocks = [gather_cores(first_blocks)]
    panels[1:] = after(panels[1:], (middle_blocks, near_by))
    ready = after(root_rows, panels[1:])
    first_halves = [root_times(index, ready, middle_blocks, 0, 2)]
    ready = after(ready, first_halves)
    first_halves.append(root_times(index, ready, middle_blocks, 1, 2))
    for panel in panels[1:]:
        if square:
            blocks, onward = gather_chips(panel, (lower_blocks, first_halves))
            ready = after(ready, onward)
        else:
            blocks = doubled_hops(panel)
        lower_blocks.append(gather_cores(blocks))
    root_sides = [root_times(index, ready, lower_blocks[0])]

    def transposed(piece, parts):
        count = piece.shape[0]
        stacked = jnp.stack(parts, axis=0)

        def columns_for(flip):
            start = (grid_index ^ flip) * middle_count
            place = (start // own_columns) ^ sibling_index
            return lax.dynamic_slice(
                stacked, (place, 0, start % own_columns), (1, count, middle_count)
            )[0]

        chips = range(0, grid_count, 2)
        other_core = swap(jnp.concatenate([columns_for(e | 1) for e in chips], axis=0), "grid", 1)
        outgoing = [
            jnp.concatenate([columns_for(e), other_core[k * count : (k + 1) * count]], axis=0)
            for k, e in enumerate(chips)
        ]
        received = outgoing[:1] + [swap(outgoing[k], "grid", 2 * k) for k in range(1, len(chips))]
        return outgoing, [part for pair in received for part in (pair[:count], pair[count:])]

    sent = [
        [half] + [swap(half, "leaf", s) for s in range(1, siblings)] for half in first_halves
    ]
    sent[0] = after(sent[0], root_sides)
    outgoing, upper_columns = transposed(first_halves[0], sent[0])
    first_side = jnp.concatenate(first_halves, axis=0)
    root_own = dot(after(first_side, outgoing), middle_rows(0))
    sent[1] = after(sent[1], root_own)
    outgoing, lower_columns = transposed(first_halves[1], sent[1])
    ready = after(root_rows, outgoing)
    root_sides += [root_times(index, ready, blocks) for blocks in lower_blocks[1:]]
    root_side = jnp.concatenate(root_sides, axis=1) - root_own
    for s in range(1, siblings):
        other = jnp.concatenate([sent[0][s], sent[1][s]], axis=0)
        root_side = root_side - dot(other, middle_rows(s))

    side_columns = [part for pair in zip(upper_columns, lower_columns) for part in pair]
    shared = middle_inverse + side_times(side_columns, middle_blocks)
    shared_parts = [shared] + [swap(shared, "leaf", s) for s in range(1, siblings)]
    side_columns = after(side_columns, shared)
    side_products = [side_times(side_columns, blocks) for blocks in lower_blocks]
    parent_side = -jnp.concatenate(side_products, axis=1)
    for s in range(siblings):
        parent_side = parent_side + dot(shared_parts[s], middle_rows(s))

    global_rows = grid_index * middle_count + jnp.arange(middle_count, dtype=jnp.int32)
    global_columns = sibling_index * own_columns + jnp.arange(own_columns, dtype=jnp.int32)
    on_diagonal = global_rows[:, None] == global_columns[None, :]
    middle_part = jnp.sum(jnp.where(on_diagonal, middle_inverse, 0.0), axis=0) + jnp.sum(
        middle_panel * first_side, axis=0
    )
    lower_rows = lax.dynamic_slice_in_dim(lower_middle, grid_index * middle_count, middle_count, 0)
    lower_part = jnp.sum(lower_panel * root_side, axis=0) + jnp.sum(
        lower_rows * parent_side, axis=0
    )

    total = jnp.concatenate([middle_part, lower_part])
    flip = 1
    while flip < grid_count:
        total = total + swap(total, "grid", flip)
        flip *= 2
    middle_total = total[:own_columns]
    lower_total = total[own_columns:]
    return (-first_side, middle_total, -root_side, -parent_side, lower_diagonal + lower_total)


def solution(mesh):
    in_specs = (
        P("grid", "leaf"),
        P("grid", "leaf"),
        P("grid", "leaf"),
        P("grid", "leaf"),
        P(None, "leaf"),
        P(),
        P("leaf"),
    )
    out_specs = (P("grid", "leaf"), P("leaf"), P("grid", "leaf"), P("grid", "leaf"), P("leaf"))
    return jax.shard_map(local, mesh=mesh, in_specs=in_specs, out_specs=out_specs, check_vma=False)
```

time: 954 us -> 406 us (0.43)
  waiting for transfers between devices: 685 us -> 175 us
  matrix products: 202 us -> 42.1 us
  Pallas kernels: 0 us -> 96.3 us
  starting transfers between devices: 0.24 us -> 29.1 us
  blocking collectives: 23 us -> 0 us
  local copies, waits for them, and re-layouts: 13.8 us -> 29.1 us
    reduce_scatter x3 -> x0, waiting for transfers between devices: 350 us -> none  [the longest x2 231 us: root_times(): lax.psum_scatter(lax.dot_general(root_rows, panel, (((0,), (0,)), ((), ()...]
    all_gather x3 -> x1, waiting for transfers between devices: 333 us -> 0.01 us  [local(): root_rows = lax.all_gather(root_inverse, 'leaf', axis=1, tiled=True)]
    ppermute x0 -> x41, waiting for transfers between devices: none -> 175 us  [swap(): return lax.ppermute(value, axis, [(i, i ^ flip) for i in range(count)])]
    dot_general x5 -> x4, matrix products: 202 us -> 42.1 us  [dot(): lax.dot_general(left, right, (((1,), (0,)), ((), ())), precision=near, pr...]
    pallas_call x0 -> x7, Pallas kernels: none -> 96.3 us  [the longest x4 63.3 us: root_times(): pl.pallas_call(functools.partial(root_kernel, count), grid_spec=pltpu.Pre...]
    ppermute x0 -> x41, starting transfers between devices: none -> 29.1 us  [swap(): return lax.ppermute(value, axis, [(i, i ^ flip) for i in range(count)])]
    psum x1 -> x0, blocking collectives: 23 us -> none  [local(): middle_total, lower_total = lax.psum((middle_part, lower_part), 'grid')]
    slice x0 -> x16, local copies, waits for them, and re-layouts: none -> 21 us  [the longest x6 10.6 us: gather_chips(): onward = [held[0][:half], held[1][half:]]]
  transfers between devices with their start and end apart: 6 -> 42, of which waited for: 6 -> 18; matrix products, arithmetic and copies ran while one was open for 15% -> 14% of each run, Pallas kernels for 0% -> 21%
where the time goes in v1:
time: 406 us; the launch traced here: 402 us
  waiting for transfers between devices  175 us (43%)
  Pallas kernels  96.3 us (24%)
  matrix products  42.1 us (10%)
  local copies, waits for them, and re-layouts  29.1 us (7%)
  starting transfers between devices  29.1 us (7%)
  other arithmetic  15.4 us (4%)
  between operations  14.9 us (4%)
    ppermute x41, waiting for transfers between devices, swap(): return lax.ppermute(value, axis, [(i, i ^ flip) for i in range(count)])  175 us
    pallas_call x4, Pallas kernels, root_times(): pl.pallas_call(functools.partial(root_kernel, count), grid_spec=pltpu.Pre...  63.3 us
    dot_general x4, matrix products, dot(): lax.dot_general(left, right, (((1,), (0,)), ((), ())), precision=near, pr...  42.1 us
    pallas_call x3, Pallas kernels, side_times(): pl.pallas_call(functools.partial(side_kernel, len(columns)), grid=(width...  33.1 us
    ppermute x41, starting transfers between devices, swap(): return lax.ppermute(value, axis, [(i, i ^ flip) for i in range(count)])  29.1 us
    slice x6, local copies, waits for them, and re-layouts, gather_chips(): onward = [held[0][:half], held[1][half:]]  10.6 us
  transfers between devices with their start and end apart: 42, of which 18 were waited for; matrix products, arithmetic and copies ran while one was open for 14% of the time, Pallas kernels for 21%

profile of v1, /device:TPU:0, one launch (start us, length us, event | category | flops | bytes accessed | tf_op | source)
XLA Modules:
  0.0 402.4 jit_solution(8219737135788676863)
XLA Ops:
  8.8 2.9 collective-permute-start.1
  11.7 1.5 collective-permute-start.3
  14.1 2.5 broadcast_multiply_fusion
  16.6 2.1 fusion.60
  19.3 39.0 %collective-permute-done.1.refs_2_.refs_18_ = f32[512,1024]{1,0:T(8,128)} collective-permute-done((f32[512,1024]{1,0:T(8,128)S(1)}, f32[512,1024]{1,0:T(8,128)}, u32[]{:S(2)}, u32[]{:S(2)}) %collective-permute-start.1) | collective-permute-done | bytes 2097184 | tf_op jit(solution)/shard_map/ppermute | solution.py:144
  58.3 2.1 collective-permute-done.3.refs_4_.refs_20_
  60.4 41.9 %collective-permute-done.9.refs_2_.refs_18_ = f32[512,1024]{1,0:T(8,128)S(1)} collective-permute-done((f32[512,1024]{1,0:T(8,128)S(1)}, f32[512,1024]{1,0:T(8,128)S(1)}, u32[]{:S(2)}, u32[]{:S(2)}) %collective-permute-start.9) | collective-permute-done | bytes 2097184 | tf_op jit(solution)/shard_map/ppermute | solution.py:144
  102.3 2.1 slice.91
  104.4 1.8 collective-permute-start.5
  106.2 1.3 slice.92
  107.7 1.6 collective-permute-start.6
  109.4 19.9 %collective-permute-done.5.refs_6_.refs_22_ = f32[256,1024]{1,0:T(8,128)S(1)} collective-permute-done((f32[256,1024]{1,0:T(8,128)S(1)}, f32[256,1024]{1,0:T(8,128)S(1)}, u32[]{:S(2)}, u32[]{:S(2)}) %collective-permute-start.5) | collective-permute-done | bytes 1048608 | tf_op jit(solution)/shard_map/ppermute | solution.py:144
  129.3 4.0 collective-permute-done.6.refs_7_.refs_23_
  133.8 1.5 slice.94
  135.2 1.1 slice.95
  136.7 1.2 copy-done.9
  137.9 1.6 collective-permute-start.18
  141.0 1.5 collective-permute-start.14
  142.5 20.3 %collective-permute-done.17.refs_6_.refs_22_ = f32[256,1024]{1,0:T(8,128)} collective-permute-done((f32[256,1024]{1,0:T(8,128)}, f32[256,1024]{1,0:T(8,128)}, u32[]{:S(2)}, u32[]{:S(2)}) %collective-permute-start.17) | collective-permute-done | bytes 1048608 | tf_op jit(solution)/shard_map/ppermute | solution.py:144
  162.8 1.5 collective-permute-done.18.refs_7_.refs_23_
  164.3 1.2 copy-done.6
  165.5 1.2 copy-done.10
  166.8 1.2 copy-done.14
  168.0 12.0 %shard_map.110 = f32[256,1024]{1,0:T(8,128)S(1)} custom-call(s32[1]{0:T(128)} %bitcast.index_ref, f32[512,4096]{1,0:T(8,128)} %all-gather.2.cloned.1.call-done.root_ref, f32[512,1024]{1,0:T(8,128)S(1)} %copy-done, f32[512,1024]{1,0:T(8,128)} %collective-permute-done.refs_1_.refs_17_, f32[512,1024]{1,0:T(8,128)} %collective-permute-done.1.refs_2_.refs_18_, ...), custom_call_target="tpu_custom_call" | custom-call | flops 6442450944 | bytes 22020096 | tf_op jit(solution)/shard_map/pallas_call | solution.py:100
  180.0 1.2 copy-done.3
  181.3 11.7 %shard_map.111 = f32[256,1024]{1,0:T(8,128)S(1)} custom-call(s32[1]{0:T(128)} %bitcast.index_ref, f32[512,4096]{1,0:T(8,128)} %all-gather.2.cloned.1.call-done.root_ref, f32[512,1024]{1,0:T(8,128)S(1)} %copy-done, f32[512,1024]{1,0:T(8,128)} %collective-permute-done.refs_1_.refs_17_, f32[512,1024]{1,0:T(8,128)} %collective-permute-done.1.refs_2_.refs_18_, ...), custom_call_target="tpu_custom_call" | custom-call | flops 6442450944 | bytes 22020096 | tf_op jit(solution)/shard_map/pallas_call | solution.py:100
  193.0 1.7 collective-permute-start.22
  194.8 13.0 %collective-permute-done.13.refs_2_.refs_18_ = f32[512,1024]{1,0:T(8,128)} collective-permute-done((f32[512,1024]{1,0:T(8,128)}, f32[512,1024]{1,0:T(8,128)}, u32[]{:S(2)}, u32[]{:S(2)}) %collective-permute-start.13) | collective-permute-done | bytes 2097184 | tf_op jit(solution)/shard_map/ppermute | solution.py:144
  207.8 2.3 slice.96
  210.1 2.3 slice.97
  212.4 19.8 %shard_map.112 = f32[512,1024]{1,0:T(8,128)S(1)} custom-call(s32[1]{0:T(128)} %bitcast.index_ref, f32[512,4096]{1,0:T(8,128)} %all-gather.2.cloned.1.call-done.root_ref, f32[512,1024]{1,0:T(8,128)S(1)} %copy-done.17, f32[512,1024]{1,0:T(8,128)} %copy-done.34, f32[512,1024]{1,0:T(8,128)} %copy-done.31, f32[512,1024]{1,0:T(8,128)} %copy-done.35, ...), custom_call_target="tpu_custom_call" | custom-call | flops 12884901888 | bytes 27262976 | tf_op jit(solution)/shard_map/pallas_call | solution.py:100
  232.2 1.3 fusion.35
  233.5 1.1 fusion.49
  236.1 1.9 collective-permute-start.21
  238.0 1.2 collective-permute-start.27
  239.2 1.5 collective-permute-start.28
  240.7 3.1 multiply_reduce_fusion.2
  243.8 2.1 fusion.63
  248.4 10.8 %fusion.6 = f32[512,2048]{1,0:T(8,128)} fusion(f32[512,1024]{1,0:T(8,128)S(1)} %get-tuple-element.49, f32[2048,2048]{1,0:T(8,128)} %param.11, s32[]{:T(128)S(6)} %select_n.206), kind=kOutput, calls=%fused_computation.6 | convolution fusion | flops 6442450944 | bytes 14680068 | tf_op jit(solution)/shard_map/dot_general | solution.py:17
  259.3 2.1 collective-permute-done.21
  261.3 1.1 fusion.19
  263.5 2.1 collective-permute-done.28.refs_7_.refs_23_
  266.4 9.2 %collective-permute-done.35 = f32[512,256]{1,0:T(8,128)} collective-permute-done((f32[512,256]{1,0:T(8,128)S(1)}, f32[512,256]{1,0:T(8,128)}, u32[]{:S(2)}, u32[]{:S(2)}) %collective-permute-start.35) | collective-permute-done | bytes 524320 | tf_op jit(solution)/shard_map/ppermute | solution.py:144
  275.6 1.5 collective-permute-start.31
  277.1 1.1 fusion.65
  278.2 8.6 %collective-permute-done.33 = f32[512,256]{1,0:T(8,128)} collective-permute-done((f32[512,256]{1,0:T(8,128)}, f32[512,256]{1,0:T(8,128)}, u32[]{:S(2)}, u32[]{:S(2)}) %collective-permute-start.33) | collective-permute-done | bytes 524320 | tf_op jit(solution)/shard_map/ppermute | solution.py:144
  286.8 1.5 collective-permute-done.31
  288.2 1.1 fusion.67
  289.3 1.1 fusion.69
  291.3 2.2 collective-permute-start.36
  295.8 19.7 %shard_map.113 = f32[512,1024]{1,0:T(8,128)S(1)} custom-call(s32[1]{0:T(128)} %bitcast.index_ref, f32[512,4096]{1,0:T(8,128)} %all-gather.2.cloned.1.call-done.root_ref, f32[512,1024]{1,0:T(8,128)} %get-tuple-element.39.refs_0_.refs_16_, f32[512,1024]{1,0:T(8,128)} %collective-permute-done.15.refs_1_.refs_17_, ...), custom_call_target="tpu_custom_call" | custom-call | flops 12884901888 | bytes 27262976 | tf_op jit(solution)/shard_map/pallas_call | solution.py:100
  315.6 14.7 %fusion.59 = (f32[512,2048]{1,0:T(8,128)}, f32[2048]{0:T(1024)S(1)}) fusion(f32[512,2048]{1,0:T(8,128)} %copy-done.22, f32[2048,2048]{1,0:T(8,128)} %param.11, s32[]{:T(128)S(6)} %select_n.207, f32[256,1024]{1,0:T(8,128)S(1)} %copy-done.26, f32[256,1024]{1,0:T(8,128)S(1)} %copy-done.24, f32[512,2048]{1,0:T(8,128)} %fusion.6, ...), kind=kOutput, calls=%fused_computation.107 | convolution fusion | flops 6449264640 | bytes 27271172 | tf_op jit(solution)/shard_map/dot_general | solution.py:17
  330.4 1.2 fusion.66
  331.6 1.1 fusion.68
  332.7 10.8 %shard_map.114 = f32[256,1024]{1,0:T(8,128)S(1)} custom-call(f32[256,256]{1,0:T(8,128)S(1)} %get-tuple-element.53.refs_0_, f32[256,256]{1,0:T(8,128)S(1)} %copy-done.20, f32[256,256]{1,0:T(8,128)S(1)} %copy-done.21, f32[256,256]{1,0:T(8,128)S(1)} %get-tuple-element.56.refs_3_, f32[256,256]{1,0:T(8,128)S(1)} %get-tuple-element.57.refs_4_, ...), custom_call_target="tpu_custom_call" | custom-call | flops 6442450944 | bytes 22020096 | tf_op jit(solution)/shard_map/pallas_call | solution.py:125
  344.2 11.2 %shard_map.115 = f32[256,1024]{1,0:T(8,128)S(1)} custom-call(f32[256,256]{1,0:T(8,128)S(1)} %get-tuple-element.53.refs_0_, f32[256,256]{1,0:T(8,128)S(1)} %copy-done.20, f32[256,256]{1,0:T(8,128)S(1)} %copy-done.21, f32[256,256]{1,0:T(8,128)S(1)} %get-tuple-element.56.refs_3_, f32[256,256]{1,0:T(8,128)S(1)} %get-tuple-element.57.refs_4_, ...), custom_call_target="tpu_custom_call" | custom-call | flops 6442450944 | bytes 22020096 | tf_op jit(solution)/shard_map/pallas_call | solution.py:125
  355.4 11.1 %shard_map.116 = f32[256,1024]{1,0:T(8,128)S(1)} custom-call(f32[256,256]{1,0:T(8,128)S(1)} %get-tuple-element.53.refs_0_, f32[256,256]{1,0:T(8,128)S(1)} %copy-done.20, f32[256,256]{1,0:T(8,128)S(1)} %copy-done.21, f32[256,256]{1,0:T(8,128)S(1)} %get-tuple-element.56.refs_3_, f32[256,256]{1,0:T(8,128)S(1)} %get-tuple-element.57.refs_4_, ...), custom_call_target="tpu_custom_call" | custom-call | flops 6442450944 | bytes 22020096 | tf_op jit(solution)/shard_map/pallas_call | solution.py:125
  366.5 2.3 collective-permute-done.37
  368.8 6.3 %fusion = f32[256,2048]{1,0:T(8,128)S(1)} fusion(f32[256,1024]{1,0:T(8,128)S(1)} %collective-permute-done.37, f32[2048,2048]{1,0:T(8,128)} %param.11, s32[]{:T(128)S(6)} %select_n.207), kind=kOutput, calls=%fused_computation | convolution fusion | flops 3221225472 | bytes 11534340 | tf_op jit(solution)/shard_map/dot_general | solution.py:17
  375.1 10.3 %fusion.61 = (f32[256,2048]{1,0:T(8,128)}, f32[2048]{0:T(1024)S(1)}) fusion(f32[2048,2048]{1,0:T(8,128)} %param.11, s32[]{:T(128)S(6)} %select_n.208, f32[256,2048]{1,0:T(8,128)S(1)} %fusion, f32[256,1024]{1,0:T(8,128)S(1)} %get-tuple-element.95, s32[]{:T(128)S(6)} %select_n.206, f32[256,1024]{1,0:T(8,128)S(1)} %shard_map.116, f32[256,1024]{1,0:T(8,128)S(1)} %shard_map.115), kind=kOutput, calls=%fused_computation.109 | convolution fusion | flops 3224893440 | bytes 17833992 | tf_op jit(solution)/shard_map/dot_general | solution.py:17
  385.5 1.2 collective-permute-done.38
  386.7 1.1 collective-permute-start.39
  387.7 2.6 collective-permute-done.39
  391.2 2.9 collective-permute-done.40
  (148 shorter events, 17.6 us)
Async XLA Ops:
  7.2 157.1 %all-gather.2.cloned.1.call-start = ((), (), s32[]{:S(2)}) async-start(), calls=%async_computation | async-start | bytes 10485760 | tf_op jit(solution)/shard_map/all_gather | solution.py:211
  8.8 49.5 %collective-permute-start.1 = (f32[512,1024]{1,0:T(8,128)S(1)}, f32[512,1024]{1,0:T(8,128)}, u32[]{:S(2)}, u32[]{:S(2)}) collective-permute-start(f32[512,1024]{1,0:T(8,128)S(1)} %copy-done), channel_id=1, source_target_pairs={{0,2},{1,3},{2,0},{3,1},{4,6},{5,7},{6,4},{7,5},{8,10},{9,11},{10,... | collective-permute-start | bytes 6291464 | tf_op jit(solution)/shard_map/ppermute | solution.py:144
  11.7 48.7 %collective-permute-start.3 = (f32[512,1024]{1,0:T(8,128)S(1)}, f32[512,1024]{1,0:T(8,128)}, u32[]{:S(2)}, u32[]{:S(2)}) collective-permute-start(f32[512,1024]{1,0:T(8,128)S(1)} %copy-done), channel_id=1, source_target_pairs={{0,4},{1,5},{2,6},{3,7},{4,0},{5,1},{6,2},{7,3},{8,12},{9,13},{10,... | collective-permute-start | bytes 6291464 | tf_op jit(solution)/shard_map/ppermute | solution.py:144
  13.2 47.1 %collective-permute-start = (f32[512,1024]{1,0:T(8,128)S(1)}, f32[512,1024]{1,0:T(8,128)}, u32[]{:S(2)}, u32[]{:S(2)}) collective-permute-start(f32[512,1024]{1,0:T(8,128)S(1)} %copy-done), channel_id=1, source_target_pairs={{0,1},{1,0},{2,3},{3,2},{4,5},{5,4},{6,7},{7,6},{8,9},{9,8},{10,11... | collective-permute-start | bytes 6291464 | tf_op jit(solution)/shard_map/ppermute | solution.py:144
  16.6 91.0 %copy-start.22 = (f32[512,2048]{1,0:T(8,128)}, f32[512,2048]{1,0:T(8,128)S(1)}, u32[]{:S(2)}) copy-start(f32[512,2048]{1,0:T(8,128)S(1)} %broadcast_multiply_fusion) | copy-start | bytes 12582916
  18.7 88.8 %copy-start.16 = (f32[512,1024]{1,0:T(8,128)}, f32[512,1024]{1,0:T(8,128)S(1)}, u32[]{:S(2)}) copy-start(f32[512,1024]{1,0:T(8,128)S(1)} %get-tuple-element.71.refs_0_.refs_16_) | copy-start | bytes 6291460
  18.7 83.5 %collective-permute-start.9 = (f32[512,1024]{1,0:T(8,128)S(1)}, f32[512,1024]{1,0:T(8,128)S(1)}, u32[]{:S(2)}, u32[]{:S(2)}) collective-permute-start(f32[512,1024]{1,0:T(8,128)S(1)} %get-tuple-element.71.refs_0_.refs_16_), channel_id=1, source_target_pairs={{0,2},{1,3},{2,0},{3,1},{4,6},{5,7},{6,4},{7,5},{8,10},{9,11},{10,... | collective-permute-start | bytes 6291464 | tf_op jit(solution)/shard_map/ppermute | solution.py:144
  19.3 88.3 %collective-permute-start.11 = (f32[512,1024]{1,0:T(8,128)S(1)}, f32[512,1024]{1,0:T(8,128)S(1)}, u32[]{:S(2)}, u32[]{:S(2)}) collective-permute-start(f32[512,1024]{1,0:T(8,128)S(1)} %get-tuple-element.71.refs_0_.refs_16_), channel_id=1, source_target_pairs={{0,4},{1,5},{2,6},{3,7},{4,0},{5,1},{6,2},{7,3},{8,12},{9,13},{10,... | collective-permute-start | bytes 6291464 | tf_op jit(solution)/shard_map/ppermute | solution.py:144
  58.3 51.0 %collective-permute-start.16 = (f32[512,1024]{1,0:T(8,128)S(1)}, f32[512,1024]{1,0:T(8,128)S(1)}, u32[]{:S(2)}, u32[]{:S(2)}) collective-permute-start(f32[512,1024]{1,0:T(8,128)S(1)} %get-tuple-element.71.refs_0_.refs_16_), channel_id=1, source_target_pairs={{0,1},{1,0},{2,3},{3,2},{4,5},{5,4},{6,7},{7,6},{8,9},{9,8},{10,11... | collective-permute-start | bytes 6291464 | tf_op jit(solution)/shard_map/ppermute | solution.py:144
  102.3 31.5 %copy-start.31 = (f32[512,1024]{1,0:T(8,128)}, f32[512,1024]{1,0:T(8,128)S(1)}, u32[]{:S(2)}) copy-start(f32[512,1024]{1,0:T(8,128)S(1)} %collective-permute-done.9.refs_2_.refs_18_) | copy-start | bytes 6291460
  102.3 31.0 %collective-permute-start.10 = (f32[512,1024]{1,0:T(8,128)S(1)}, f32[512,1024]{1,0:T(8,128)S(1)}, u32[]{:S(2)}, u32[]{:S(2)}) collective-permute-start(f32[512,1024]{1,0:T(8,128)S(1)} %collective-permute-done.9.refs_2_.refs_18_), channel_id=1, source_target_pairs={{0,1},{1,0},{2,3},{3,2},{4,5},{5,4},{6,7},{7,6},{8,9},{9,8},{10,11... | collective-permute-start | bytes 6291464 | tf_op jit(solution)/shard_map/ppermute | solution.py:144
  104.4 24.9 %collective-permute-start.5 = (f32[256,1024]{1,0:T(8,128)S(1)}, f32[256,1024]{1,0:T(8,128)S(1)}, u32[]{:S(2)}, u32[]{:S(2)}) collective-permute-start(f32[256,1024]{1,0:T(8,128)S(1)} %slice.91), channel_id=1, source_target_pairs={{0,4},{1,5},{2,6},{3,7},{4,0},{5,1},{6,2},{7,3},{8,12},{9,13},{10,... | collective-permute-start | bytes 3145736 | tf_op jit(solution)/shard_map/ppermute | solution.py:144
  107.6 28.8 %copy-start.32 = (f32[512,1024]{1,0:T(8,128)}, f32[512,1024]{1,0:T(8,128)S(1)}, u32[]{:S(2)}) copy-start(f32[512,1024]{1,0:T(8,128)S(1)} %collective-permute-done.11.refs_4_.refs_20_) | copy-start | bytes 6291460
  107.6 28.8 %collective-permute-start.12 = (f32[512,1024]{1,0:T(8,128)S(1)}, f32[512,1024]{1,0:T(8,128)S(1)}, u32[]{:S(2)}, u32[]{:S(2)}) collective-permute-start(f32[512,1024]{1,0:T(8,128)S(1)} %collective-permute-done.11.refs_4_.refs_20_), channel_id=1, source_target_pairs={{0,1},{1,0},{2,3},{3,2},{4,5},{5,4},{6,7},{7,6},{8,9},{9,8},{10,11... | collective-permute-start | bytes 6291464 | tf_op jit(solution)/shard_map/ppermute | solution.py:144
  107.7 25.6 %collective-permute-start.6 = (f32[256,1024]{1,0:T(8,128)S(1)}, f32[256,1024]{1,0:T(8,128)S(1)}, u32[]{:S(2)}, u32[]{:S(2)}) collective-permute-start(f32[256,1024]{1,0:T(8,128)S(1)} %slice.92), channel_id=1, source_target_pairs={{0,2},{1,3},{2,0},{3,1},{4,6},{5,7},{6,4},{7,5},{8,10},{9,11},{10,... | collective-permute-start | bytes 3145736 | tf_op jit(solution)/shard_map/ppermute | solution.py:144
  109.2 30.3 %copy-start.34 = (f32[512,1024]{1,0:T(8,128)}, f32[512,1024]{1,0:T(8,128)S(1)}, u32[]{:S(2)}) copy-start(f32[512,1024]{1,0:T(8,128)S(1)} %collective-permute-done.16.refs_1_.refs_17_) | copy-start | bytes 6291460
  109.2 31.3 %collective-permute-start.2 = (f32[512,1024]{1,0:T(8,128)}, f32[512,1024]{1,0:T(8,128)}, u32[]{:S(2)}, u32[]{:S(2)}) collective-permute-start(f32[512,1024]{1,0:T(8,128)} %collective-permute-done.1.refs_2_.refs_18_), channel_id=1, source_target_pairs={{0,1},{1,0},{2,3},{3,2},{4,5},{5,4},{6,7},{7,6},{8,9},{9,8},{10,11... | collective-permute-start | bytes 6291464 | tf_op jit(solution)/shard_map/ppermute | solution.py:144
  129.3 35.0 %copy-start.2 = (f32[256,1024]{1,0:T(8,128)}, f32[256,1024]{1,0:T(8,128)S(1)}, u32[]{:S(2)}) copy-start(f32[256,1024]{1,0:T(8,128)S(1)} %collective-permute-done.5.refs_6_.refs_22_) | copy-start | bytes 3145732
  129.3 11.2 %collective-permute-start.4 = (f32[512,1024]{1,0:T(8,128)}, f32[512,1024]{1,0:T(8,128)}, u32[]{:S(2)}, u32[]{:S(2)}) collective-permute-start(f32[512,1024]{1,0:T(8,128)} %collective-permute-done.3.refs_4_.refs_20_), channel_id=1, source_target_pairs={{0,1},{1,0},{2,3},{3,2},{4,5},{5,4},{6,7},{7,6},{8,9},{9,8},{10,11... | collective-permute-start | bytes 6291464 | tf_op jit(solution)/shard_map/ppermute | solution.py:144
  133.2 3.1 copy-start.5
  133.2 3.4 collective-permute-start.7
  133.2 7.3 %copy-start.35 = (f32[512,1024]{1,0:T(8,128)}, f32[512,1024]{1,0:T(8,128)S(1)}, u32[]{:S(2)}) copy-start(f32[512,1024]{1,0:T(8,128)S(1)} %collective-permute-done.10.refs_3_.refs_19_) | copy-start | bytes 6291460
  133.3 6.3 %collective-permute-start.8 = (f32[256,1024]{1,0:T(8,128)S(1)}, f32[256,1024]{1,0:T(8,128)S(1)}, u32[]{:S(2)}, u32[]{:S(2)}) collective-permute-start(f32[256,1024]{1,0:T(8,128)S(1)} %collective-permute-done.6.refs_7_.refs_23_), channel_id=1, source_target_pairs={{0,1},{1,0},{2,3},{3,2},{4,5},{5,4},{6,7},{7,6},{8,9},{9,8},{10,11... | collective-permute-start | bytes 3145736 | tf_op jit(solution)/shard_map/ppermute | solution.py:144
  136.3 4.2 %copy-start.36 = (f32[512,1024]{1,0:T(8,128)}, f32[512,1024]{1,0:T(8,128)S(1)}, u32[]{:S(2)}) copy-start(f32[512,1024]{1,0:T(8,128)S(1)} %collective-permute-done.12.refs_5_.refs_21_) | copy-start | bytes 6291460
  136.4 26.4 %collective-permute-start.17 = (f32[256,1024]{1,0:T(8,128)}, f32[256,1024]{1,0:T(8,128)}, u32[]{:S(2)}, u32[]{:S(2)}) collective-permute-start(f32[256,1024]{1,0:T(8,128)} %slice.94), channel_id=1, source_target_pairs={{0,4},{1,5},{2,6},{3,7},{4,0},{5,1},{6,2},{7,3},{8,12},{9,13},{10,... | collective-permute-start | bytes 3145736 | tf_op jit(solution)/shard_map/ppermute | solution.py:144
  137.9 26.4 %collective-permute-start.18 = (f32[256,1024]{1,0:T(8,128)}, f32[256,1024]{1,0:T(8,128)}, u32[]{:S(2)}, u32[]{:S(2)}) collective-permute-start(f32[256,1024]{1,0:T(8,128)} %slice.95), channel_id=1, source_target_pairs={{0,2},{1,3},{2,0},{3,1},{4,6},{5,7},{6,4},{7,5},{8,10},{9,11},{10,... | collective-permute-start | bytes 3145736 | tf_op jit(solution)/shard_map/ppermute | solution.py:144
  140.5 67.3 %collective-permute-start.13 = (f32[512,1024]{1,0:T(8,128)}, f32[512,1024]{1,0:T(8,128)}, u32[]{:S(2)}, u32[]{:S(2)}) collective-permute-start(f32[512,1024]{1,0:T(8,128)} %get-tuple-element.39.refs_0_.refs_16_), channel_id=1, source_target_pairs={{0,2},{1,3},{2,0},{3,1},{4,6},{5,7},{6,4},{7,5},{8,10},{9,11},{10,... | collective-permute-start | bytes 6291464 | tf_op jit(solution)/shard_map/ppermute | solution.py:144
  141.0 66.8 %collective-permute-start.14 = (f32[512,1024]{1,0:T(8,128)}, f32[512,1024]{1,0:T(8,128)}, u32[]{:S(2)}, u32[]{:S(2)}) collective-permute-start(f32[512,1024]{1,0:T(8,128)} %get-tuple-element.39.refs_0_.refs_16_), channel_id=1, source_target_pairs={{0,4},{1,5},{2,6},{3,7},{4,0},{5,1},{6,2},{7,3},{8,12},{9,13},{10,... | collective-permute-start | bytes 6291464 | tf_op jit(solution)/shard_map/ppermute | solution.py:144
  142.5 65.3 %collective-permute-start.15 = (f32[512,1024]{1,0:T(8,128)}, f32[512,1024]{1,0:T(8,128)}, u32[]{:S(2)}, u32[]{:S(2)}) collective-permute-start(f32[512,1024]{1,0:T(8,128)} %get-tuple-element.39.refs_0_.refs_16_), channel_id=1, source_target_pairs={{0,1},{1,0},{2,3},{3,2},{4,5},{5,4},{6,7},{7,6},{8,9},{9,8},{10,11... | collective-permute-start | bytes 6291464 | tf_op jit(solution)/shard_map/ppermute | solution.py:144
  162.8 30.2 %collective-permute-start.19 = (f32[256,1024]{1,0:T(8,128)}, f32[256,1024]{1,0:T(8,128)}, u32[]{:S(2)}, u32[]{:S(2)}) collective-permute-start(f32[256,1024]{1,0:T(8,128)} %collective-permute-done.17.refs_6_.refs_22_), channel_id=1, source_target_pairs={{0,1},{1,0},{2,3},{3,2},{4,5},{5,4},{6,7},{7,6},{8,9},{9,8},{10,11... | collective-permute-start | bytes 3145736 | tf_op jit(solution)/shard_map/ppermute | solution.py:144
  164.3 30.5 %collective-permute-start.20 = (f32[256,1024]{1,0:T(8,128)}, f32[256,1024]{1,0:T(8,128)}, u32[]{:S(2)}, u32[]{:S(2)}) collective-permute-start(f32[256,1024]{1,0:T(8,128)} %collective-permute-done.18.refs_7_.refs_23_), channel_id=1, source_target_pairs={{0,1},{1,0},{2,3},{3,2},{4,5},{5,4},{6,7},{7,6},{8,9},{9,8},{10,11... | collective-permute-start | bytes 3145736 | tf_op jit(solution)/shard_map/ppermute | solution.py:144
  168.0 12.0 %copy-start.7 = (f32[256,1024]{1,0:T(8,128)S(1)}, f32[256,1024]{1,0:T(8,128)}, u32[]{:S(2)}) copy-start(f32[256,1024]{1,0:T(8,128)} %copy-done.5) | copy-start | bytes 3145732
  168.0 12.0 %copy-start.11 = (f32[256,1024]{1,0:T(8,128)S(1)}, f32[256,1024]{1,0:T(8,128)}, u32[]{:S(2)}) copy-start(f32[256,1024]{1,0:T(8,128)} %copy-done.9) | copy-start | bytes 3145732
  181.3 52.2 %copy-start.1 = (f32[256,1024]{1,0:T(8,128)}, f32[256,1024]{1,0:T(8,128)S(1)}, u32[]{:S(2)}) copy-start(f32[256,1024]{1,0:T(8,128)S(1)} %shard_map.110) | copy-start | bytes 3145732
  193.0 19.4 %copy-start.17 = (f32[512,1024]{1,0:T(8,128)S(1)}, f32[512,1024]{1,0:T(8,128)}, u32[]{:S(2)}) copy-start(f32[512,1024]{1,0:T(8,128)} %copy-done.16) | copy-start | bytes 6291460
  193.0 39.1 %collective-permute-start.22 = (f32[256,1024]{1,0:T(8,128)S(1)}, f32[256,1024]{1,0:T(8,128)S(1)}, u32[]{:S(2)}, u32[]{:S(2)}) collective-permute-start(f32[256,1024]{1,0:T(8,128)S(1)} %shard_map.110), channel_id=1, source_target_pairs={{0,8},{8,0},{16,24},{24,16},{1,9},{9,1},{17,25},{25,17},{2,10},{10... | collective-permute-start | bytes 3145736 | tf_op jit(solution)/shard_map/ppermute | solution.py:144
  235.6 8.2 %collective-permute-start.23 = (f32[1024,256]{1,0:T(8,128)}, f32[1024,256]{1,0:T(8,128)}, u32[]{:S(2)}, u32[]{:S(2)}) collective-permute-start(f32[1024,256]{1,0:T(8,128)} %pad_maximum_fusion.1), channel_id=1, source_target_pairs={{0,1},{1,0},{2,3},{3,2},{4,5},{5,4},{6,7},{7,6},{8,9},{9,8},{10,11... | collective-permute-start | bytes 3145736 | tf_op jit(solution)/shard_map/ppermute | solution.py:144
  235.6 58.8 %collective-permute-start.25 = (f32[512,1024]{1,0:T(8,128)}, f32[512,1024]{1,0:T(8,128)}, u32[]{:S(2)}, u32[]{:S(2)}) collective-permute-start(f32[512,1024]{1,0:T(8,128)} %collective-permute-done.13.refs_2_.refs_18_), channel_id=1, source_target_pairs={{0,1},{1,0},{2,3},{3,2},{4,5},{5,4},{6,7},{7,6},{8,9},{9,8},{10,11... | collective-permute-start | bytes 6291464 | tf_op jit(solution)/shard_map/ppermute | solution.py:144
  236.1 25.2 %collective-permute-start.21 = (f32[256,1024]{1,0:T(8,128)S(1)}, f32[256,1024]{1,0:T(8,128)S(1)}, u32[]{:S(2)}, u32[]{:S(2)}) collective-permute-start(f32[256,1024]{1,0:T(8,128)S(1)} %shard_map.111), channel_id=1, source_target_pairs={{0,8},{8,0},{16,24},{24,16},{1,9},{9,1},{17,25},{25,17},{2,10},{10... | collective-permute-start | bytes 3145736 | tf_op jit(solution)/shard_map/ppermute | solution.py:144
  238.0 25.5 %collective-permute-start.27 = (f32[256,1024]{1,0:T(8,128)}, f32[256,1024]{1,0:T(8,128)}, u32[]{:S(2)}, u32[]{:S(2)}) collective-permute-start(f32[256,1024]{1,0:T(8,128)} %slice.96), channel_id=1, source_target_pairs={{0,4},{1,5},{2,6},{3,7},{4,0},{5,1},{6,2},{7,3},{8,12},{9,13},{10,... | collective-permute-start | bytes 3145736 | tf_op jit(solution)/shard_map/ppermute | solution.py:144
  239.2 26.4 %collective-permute-start.28 = (f32[256,1024]{1,0:T(8,128)}, f32[256,1024]{1,0:T(8,128)}, u32[]{:S(2)}, u32[]{:S(2)}) collective-permute-start(f32[256,1024]{1,0:T(8,128)} %slice.97), channel_id=1, source_target_pairs={{0,2},{1,3},{2,0},{3,1},{4,6},{5,7},{6,4},{7,5},{8,10},{9,11},{10,... | collective-permute-start | bytes 3145736 | tf_op jit(solution)/shard_map/ppermute | solution.py:144
  243.8 3.8 copy-start.28
  245.9 29.7 %collective-permute-start.35 = (f32[512,256]{1,0:T(8,128)S(1)}, f32[512,256]{1,0:T(8,128)}, u32[]{:S(2)}, u32[]{:S(2)}) collective-permute-start(f32[512,256]{1,0:T(8,128)S(1)} %pad_maximum_fusion.5), channel_id=1, source_target_pairs={{0,6},{1,7},{2,4},{3,5},{4,2},{5,3},{6,0},{7,1},{8,14},{9,15},{10,... | collective-permute-start | bytes 1572872 | tf_op jit(solution)/shard_map/ppermute | solution.py:144
  261.3 33.9 %collective-permute-start.26 = (f32[512,1024]{1,0:T(8,128)}, f32[512,1024]{1,0:T(8,128)}, u32[]{:S(2)}, u32[]{:S(2)}) collective-permute-start(f32[512,1024]{1,0:T(8,128)} %collective-permute-done.14.refs_4_.refs_20_), channel_id=1, source_target_pairs={{0,1},{1,0},{2,3},{3,2},{4,5},{5,4},{6,7},{7,6},{8,9},{9,8},{10,11... | collective-permute-start | bytes 6291464 | tf_op jit(solution)/shard_map/ppermute | solution.py:144
  263.5 26.9 %collective-permute-start.24 = (f32[1024,256]{1,0:T(8,128)S(1)}, f32[1024,256]{1,0:T(8,128)S(1)}, u32[]{:S(2)}, u32[]{:S(2)}) collective-permute-start(f32[1024,256]{1,0:T(8,128)S(1)} %pad_maximum_fusion.2), channel_id=1, source_target_pairs={{0,1},{1,0},{2,3},{3,2},{4,5},{5,4},{6,7},{7,6},{8,9},{9,8},{10,11... | collective-permute-start | bytes 3145736 | tf_op jit(solution)/shard_map/ppermute | solution.py:144
  265.7 21.1 %collective-permute-start.33 = (f32[512,256]{1,0:T(8,128)}, f32[512,256]{1,0:T(8,128)}, u32[]{:S(2)}, u32[]{:S(2)}) collective-permute-start(f32[512,256]{1,0:T(8,128)} %pad_maximum_fusion.4), channel_id=1, source_target_pairs={{0,4},{1,5},{2,6},{3,7},{4,0},{5,1},{6,2},{7,3},{8,12},{9,13},{10,... | collective-permute-start | bytes 1572872 | tf_op jit(solution)/shard_map/ppermute | solution.py:144
  275.6 12.6 %collective-permute-start.31 = (f32[512,256]{1,0:T(8,128)}, f32[512,256]{1,0:T(8,128)}, u32[]{:S(2)}, u32[]{:S(2)}) collective-permute-start(f32[512,256]{1,0:T(8,128)} %pad_maximum_fusion.3), channel_id=1, source_target_pairs={{0,2},{1,3},{2,0},{3,1},{4,6},{5,7},{6,4},{7,5},{8,10},{9,11},{10,... | collective-permute-start | bytes 1572872 | tf_op jit(solution)/shard_map/ppermute | solution.py:144
  286.8 9.0 %collective-permute-start.29 = (f32[256,1024]{1,0:T(8,128)}, f32[256,1024]{1,0:T(8,128)S(1)}, u32[]{:S(2)}, u32[]{:S(2)}) collective-permute-start(f32[256,1024]{1,0:T(8,128)} %collective-permute-done.27.refs_6_.refs_22_), channel_id=1, source_target_pairs={{0,1},{1,0},{2,3},{3,2},{4,5},{5,4},{6,7},{7,6},{8,9},{9,8},{10,11... | collective-permute-start | bytes 3145736 | tf_op jit(solution)/shard_map/ppermute | solution.py:144
  288.2 7.5 %collective-permute-start.30 = (f32[256,1024]{1,0:T(8,128)}, f32[256,1024]{1,0:T(8,128)S(1)}, u32[]{:S(2)}, u32[]{:S(2)}) collective-permute-start(f32[256,1024]{1,0:T(8,128)} %collective-permute-done.28.refs_7_.refs_23_), channel_id=1, source_target_pairs={{0,1},{1,0},{2,3},{3,2},{4,5},{5,4},{6,7},{7,6},{8,9},{9,8},{10,11... | collective-permute-start | bytes 3145736 | tf_op jit(solution)/shard_map/ppermute | solution.py:144
  291.3 39.0 %collective-permute-start.36 = (f32[512,256]{1,0:T(8,128)}, f32[512,256]{1,0:T(8,128)S(1)}, u32[]{:S(2)}, u32[]{:S(2)}) collective-permute-start(f32[512,256]{1,0:T(8,128)} %pad_maximum_fusion.8), channel_id=1, source_target_pairs={{0,6},{1,7},{2,4},{3,5},{4,2},{5,3},{6,0},{7,1},{8,14},{9,15},{10,... | collective-permute-start | bytes 1572872 | tf_op jit(solution)/shard_map/ppermute | solution.py:144
  294.4 21.2 %copy-start.19 = (f32[512,1024]{1,0:T(8,128)S(1)}, f32[512,1024]{1,0:T(8,128)}, u32[]{:S(2)}) copy-start(f32[512,1024]{1,0:T(8,128)} %copy-done.18) | copy-start | bytes 6291460
  294.4 21.2 %copy-start.24 = (f32[256,1024]{1,0:T(8,128)S(1)}, f32[256,1024]{1,0:T(8,128)}, u32[]{:S(2)}) copy-start(f32[256,1024]{1,0:T(8,128)} %copy-done.23) | copy-start | bytes 3145732
  294.4 21.2 %copy-start.26 = (f32[256,1024]{1,0:T(8,128)S(1)}, f32[256,1024]{1,0:T(8,128)}, u32[]{:S(2)}) copy-start(f32[256,1024]{1,0:T(8,128)} %copy-done.25) | copy-start | bytes 3145732
  294.4 36.0 %collective-permute-start.34 = (f32[512,256]{1,0:T(8,128)}, f32[512,256]{1,0:T(8,128)}, u32[]{:S(2)}, u32[]{:S(2)}) collective-permute-start(f32[512,256]{1,0:T(8,128)} %pad_maximum_fusion.7), channel_id=1, source_target_pairs={{0,4},{1,5},{2,6},{3,7},{4,0},{5,1},{6,2},{7,3},{8,12},{9,13},{10,... | collective-permute-start | bytes 1572872 | tf_op jit(solution)/shard_map/ppermute | solution.py:144
  295.2 36.4 %collective-permute-start.32 = (f32[512,256]{1,0:T(8,128)S(1)}, f32[512,256]{1,0:T(8,128)}, u32[]{:S(2)}, u32[]{:S(2)}) collective-permute-start(f32[512,256]{1,0:T(8,128)S(1)} %pad_maximum_fusion.6), channel_id=1, source_target_pairs={{0,2},{1,3},{2,0},{3,1},{4,6},{5,7},{6,4},{7,5},{8,10},{9,11},{10,... | collective-permute-start | bytes 1572872 | tf_op jit(solution)/shard_map/ppermute | solution.py:144
  315.6 17.1 %copy-start.15 = (f32[256,1024]{1,0:T(8,128)S(1)}, f32[256,1024]{1,0:T(8,128)}, u32[]{:S(2)}) copy-start(f32[256,1024]{1,0:T(8,128)} %copy-done.13) | copy-start | bytes 3145732
  315.6 17.1 %copy-start.20 = (f32[256,256]{1,0:T(8,128)S(1)}, f32[256,256]{1,0:T(8,128)}, u32[]{:S(2)}) copy-start(f32[256,256]{1,0:T(8,128)} %get-tuple-element.54.refs_1_) | copy-start | bytes 786436
  315.6 17.1 %copy-start.21 = (f32[256,256]{1,0:T(8,128)S(1)}, f32[256,256]{1,0:T(8,128)}, u32[]{:S(2)}) copy-start(f32[256,256]{1,0:T(8,128)} %get-tuple-element.55.refs_2_) | copy-start | bytes 786436
  332.7 10.8 %copy-start.27 = (f32[256,1024]{1,0:T(8,128)S(1)}, f32[256,1024]{1,0:T(8,128)}, u32[]{:S(2)}) copy-start(f32[256,1024]{1,0:T(8,128)} %param.8) | copy-start | bytes 3145732
  343.7 25.1 %collective-permute-start.37 = (f32[256,1024]{1,0:T(8,128)S(1)}, f32[256,1024]{1,0:T(8,128)S(1)}, u32[]{:S(2)}, u32[]{:S(2)}) collective-permute-start(f32[256,1024]{1,0:T(8,128)S(1)} %get-tuple-element.95), channel_id=1, source_target_pairs={{0,8},{8,0},{16,24},{24,16},{1,9},{9,1},{17,25},{25,17},{2,10},{10... | collective-permute-start | bytes 3145736 | tf_op jit(solution)/shard_map/ppermute | solution.py:144
  375.1 19.6 %copy-start.33 = (f32[2048]{0:T(1024)S(1)}, f32[2048]{0:T(1024)}, u32[]{:S(2)}) copy-start(f32[2048]{0:T(1024)} %param.13) | copy-start | bytes 24580
  385.4 1.2 collective-permute-start.38
  386.7 3.7 collective-permute-start.39
  390.4 3.7 collective-permute-start.40
  (15 other events, 27.1 us)
Sparse Core Ops, SparseCore 0:
  9.6 152.3 all-gather.1

commit v2 on v1

--- a/solution.py
+++ b/solution.py
@@ -10,13 +10,7 @@
 BLK = 128
 
 
-near = lax.Precision.HIGH
-
-
-def dot(left, right):
-    return lax.dot_general(
-        left, right, (((1,), (0,)), ((), ())), precision=near, preferred_element_type=jnp.float32
-    )
+unhidden = pl.CostEstimate(flops=0, transcendentals=0, bytes_accessed=0)
 
 
 def split(value):
@@ -61,14 +55,67 @@
 
     @pl.when(pl.program_id(0) == 0)
     def _():
-        start = 0
-        for column_ref in column_refs:
-            place = slice(start, start + column_ref.shape[0])
-            start += column_ref.shape[0]
-            side_high[:, place], side_low[:, place] = split(column_ref[...].T)
+        rows = column_refs[0].shape[0] // 2
+        for j, column_ref in enumerate(column_refs):
+            for core in range(2):
+                start = (2 * (j // 2) + core) * 2 * rows + (j % 2) * rows
+                place = slice(start, start + rows)
+                side_high[:, place], side_low[:, place] = split(
+                    column_ref[core * rows : (core + 1) * rows, :].T
+                )
 
     split_blocks(block_refs, high, low)
     out_ref[...] = split_dot(side_high[...], side_low[...], high[...], low[...])
+
+
+def pick_kernel(parts, spot_ref, *refs):
+    part_refs, out_refs = refs[:parts], refs[parts:]
+    rows = part_refs[0].shape[0]
+    width = out_refs[0].shape[1]
+    spots = out_refs[0].shape[0] // rows
+    for j in range(2 * spots):
+        band = slice((j // 2) * rows, (j // 2 + 1) * rows)
+        column = pl.multiple_of(spot_ref[2 * j + 1], width)
+        for s in range(parts):
+
+            @pl.when(spot_ref[2 * j] == s)
+            def _():
+                out_refs[j % 2][band, :] = part_refs[s][:, pl.ds(column, width)]
+
+
+def pick(spots, parts, width):
+    rows = parts[0].shape[0]
+    shape = jax.ShapeDtypeStruct((spots.shape[0] // 4 * rows, width), jnp.float32)
+    whole = pl.BlockSpec(memory_space=pltpu.VMEM)
+    return pl.pallas_call(
+        functools.partial(pick_kernel, len(parts)),
+        in_specs=[pl.BlockSpec(memory_space=pltpu.SMEM)] + [whole] * len(parts),
+        out_specs=[whole, whole],
+        out_shape=[shape, shape],
+        compiler_params=pltpu.CompilerParams(vmem_limit_bytes=32 * 2**20),
+        cost_estimate=unhidden,
+    )(spots, *parts)
+
+
+def pair_kernel(kept_ref, taken_ref, *out_refs):
+    rows = out_refs[0].shape[0] // 2
+    for k, out_ref in enumerate(out_refs):
+        band = slice(k * rows, (k + 1) * rows)
+        out_ref[:rows, :] = kept_ref[band, :]
+        out_ref[rows:, :] = taken_ref[band, :]
+
+
+def pair(kept, taken, count):
+    shape = jax.ShapeDtypeStruct((2 * kept.shape[0] // count, kept.shape[1]), jnp.float32)
+    whole = pl.BlockSpec(memory_space=pltpu.VMEM)
+    return pl.pallas_call(
+        pair_kernel,
+        in_specs=[whole, whole],
+        out_specs=[whole] * count,
+        out_shape=[shape] * count,
+        compiler_params=pltpu.CompilerParams(vmem_limit_bytes=32 * 2**20),
+        cost_estimate=unhidden,
+    )(kept, taken)
 
 
 def panel_scratch(height, depth, tile):
@@ -78,14 +125,6 @@
         pltpu.VMEM((depth, tile), jnp.bfloat16),
         pltpu.VMEM((depth, tile), jnp.bfloat16),
     ]
-
-
-def panel_cost(height, depth, width):
-    return pl.CostEstimate(
-        flops=6 * height * depth * width,
-        transcendentals=0,
-        bytes_accessed=4 * (height * depth + depth * width + height * width),
-    )
 
 
 def whole_spec(array, index):
@@ -113,7 +152,7 @@
         ),
         out_shape=jax.ShapeDtypeStruct((height, width), jnp.float32),
         compiler_params=pltpu.CompilerParams(vmem_limit_bytes=44 * 2**20),
-        cost_estimate=panel_cost(height, depth, width),
+        cost_estimate=unhidden,
     )(index, root_rows, *blocks)
 
 
@@ -131,8 +170,51 @@
         scratch_shapes=panel_scratch(height, depth, tile),
         out_shape=jax.ShapeDtypeStruct((height, width), jnp.float32),
         compiler_params=pltpu.CompilerParams(vmem_limit_bytes=44 * 2**20),
-        cost_estimate=panel_cost(height, depth, width),
+        cost_estimate=unhidden,
     )(*columns, *blocks)
+
+
+def mixed_kernel(parts, pieces, places_ref, *refs):
+    left_refs, right_refs, out_ref = refs[: parts * pieces], refs[parts * pieces : -5], refs[-5]
+    left_high, left_low, high, low = refs[-4:]
+
+    @pl.when(pl.program_id(0) == 0)
+    def _():
+        for s in range(parts):
+            top = 0
+            for left_ref in left_refs[s * pieces : (s + 1) * pieces]:
+                count, depth = left_ref.shape
+                band, place = slice(top, top + count), slice(s * depth, (s + 1) * depth)
+                left_high[band, place], left_low[band, place] = split(left_ref[...])
+                top += count
+
+    split_blocks(right_refs, high, low)
+    out_ref[...] = split_dot(left_high[...], left_low[...], high[...], low[...])
+
+
+def mixed_times(places, left, right):
+    height = sum(piece.shape[0] for piece in left[0])
+    own = left[0][0].shape[1]
+    depth, width = right.shape
+    tile = min(width, 256)
+
+    def band(s):
+        return pl.BlockSpec((own, tile), lambda i, places: (places[s], i))
+
+    return pl.pallas_call(
+        functools.partial(mixed_kernel, len(left), len(left[0])),
+        grid_spec=pltpu.PrefetchScalarGridSpec(
+            num_scalar_prefetch=1,
+            grid=(width // tile,),
+            in_specs=[whole_spec(piece, lambda i, p: (0, 0)) for part in left for piece in part]
+            + [band(s) for s in range(len(left))],
+            out_specs=pl.BlockSpec((height, tile), lambda i, p: (0, i)),
+            scratch_shapes=panel_scratch(height, depth, tile),
+        ),
+        out_shape=jax.ShapeDtypeStruct((height, width), jnp.float32),
+        compiler_params=pltpu.CompilerParams(vmem_limit_bytes=44 * 2**20),
+        cost_estimate=unhidden,
+    )(places, *[piece for part in left for piece in part], *[right] * len(left))
 
 
 def after(value, other):
@@ -197,10 +279,7 @@
     chunk = min(width, 1024)
     chunks = range(width // chunk)
 
-    def middle_rows(s):
-        return lax.dynamic_slice_in_dim(
-            lower_middle, (sibling_index ^ s) * own_columns, own_columns, 0
-        )
+    places = jnp.stack([sibling_index ^ s for s in range(siblings)]).astype(jnp.int32)
 
     blocks_here = local_rows // BLK
     pattern = lax.dynamic_slice(
@@ -220,63 +299,58 @@
     middle_blocks = gather_cores(middle_blocks)
     lower_blocks = [gather_cores(first_blocks)]
     panels[1:] = after(panels[1:], (middle_blocks, near_by))
-    ready = after(root_rows, panels[1:])
+    ready = after(root_rows, (panels[1:], lower_blocks))
     first_halves = [root_times(index, ready, middle_blocks, 0, 2)]
     ready = after(ready, first_halves)
     first_halves.append(root_times(index, ready, middle_blocks, 1, 2))
+    arrived = [first_halves[1]]
     for panel in panels[1:]:
         if square:
-            blocks, onward = gather_chips(panel, (lower_blocks, first_halves))
-            ready = after(ready, onward)
+            blocks, _ = gather_chips(panel, (lower_blocks, first_halves))
+            arrived += [blocks[e] for e in (1, 2, 4)]
         else:
             blocks = doubled_hops(panel)
         lower_blocks.append(gather_cores(blocks))
-    root_sides = [root_times(index, ready, lower_blocks[0])]
-
-    def transposed(piece, parts):
-        count = piece.shape[0]
-        stacked = jnp.stack(parts, axis=0)
-
-        def columns_for(flip):
-            start = (grid_index ^ flip) * middle_count
-            place = (start // own_columns) ^ sibling_index
-            return lax.dynamic_slice(
-                stacked, (place, 0, start % own_columns), (1, count, middle_count)
-            )[0]
-
-        chips = range(0, grid_count, 2)
-        other_core = swap(jnp.concatenate([columns_for(e | 1) for e in chips], axis=0), "grid", 1)
-        outgoing = [
-            jnp.concatenate([columns_for(e), other_core[k * count : (k + 1) * count]], axis=0)
-            for k, e in enumerate(chips)
+
+    spots = []
+    for e in range(grid_count):
+        start = (grid_index ^ e) * middle_count
+        spots += [(start // own_columns) ^ sibling_index, start % own_columns]
+    spots = jnp.stack(spots).astype(jnp.int32)
+
+    def transposed(parts):
+        kept, other = pick(spots, parts, middle_count)
+        outgoing = pair(kept, swap(other, "grid", 1), grid_count // 2)
+        return outgoing, [outgoing[0]] + [
+            swap(outgoing[k], "grid", 2 * k) for k in range(1, len(outgoing))
         ]
-        received = outgoing[:1] + [swap(outgoing[k], "grid", 2 * k) for k in range(1, len(chips))]
-        return outgoing, [part for pair in received for part in (pair[:count], pair[count:])]
 
     sent = [
         [half] + [swap(half, "leaf", s) for s in range(1, siblings)] for half in first_halves
     ]
-    sent[0] = after(sent[0], root_sides)
-    outgoing, upper_columns = transposed(first_halves[0], sent[0])
+    sent[0] = after(sent[0], arrived)
+    outgoing, upper_columns = transposed(sent[0])
+    ready = after(root_rows, outgoing)
+    root_sides = [root_times(index, ready, lower_blocks[0])]
+    sent[1] = after(sent[1], root_sides)
+    outgoing, lower_columns = transposed(sent[1])
     first_side = jnp.concatenate(first_halves, axis=0)
-    root_own = dot(after(first_side, outgoing), middle_rows(0))
-    sent[1] = after(sent[1], root_own)
-    outgoing, lower_columns = transposed(first_halves[1], sent[1])
-    ready = after(root_rows, outgoing)
+    left = [[sent[0][s], sent[1][s]] for s in range(siblings)]
+    mixed = mixed_times(places, after(left, outgoing), lower_middle)
+    ready = after(root_rows, mixed)
     root_sides += [root_times(index, ready, blocks) for blocks in lower_blocks[1:]]
-    root_side = jnp.concatenate(root_sides, axis=1) - root_own
-    for s in range(1, siblings):
-        other = jnp.concatenate([sent[0][s], sent[1][s]], axis=0)
-        root_side = root_side - dot(other, middle_rows(s))
+    root_side = jnp.concatenate(root_sides, axis=1) - mixed
 
     side_columns = [part for pair in zip(upper_columns, lower_columns) for part in pair]
+    side_columns = after(side_columns, root_sides)
     shared = middle_inverse + side_times(side_columns, middle_blocks)
-    shared_parts = [shared] + [swap(shared, "leaf", s) for s in range(1, siblings)]
+    shared_parts = [[shared]] + [[swap(shared, "leaf", s)] for s in range(1, siblings)]
     side_columns = after(side_columns, shared)
     side_products = [side_times(side_columns, blocks) for blocks in lower_blocks]
-    parent_side = -jnp.concatenate(side_products, axis=1)
-    for s in range(siblings):
-        parent_side = parent_side + dot(shared_parts[s], middle_rows(s))
+    shared_parts = after(shared_parts, side_products)
+    parent_side = mixed_times(places, shared_parts, lower_middle) - jnp.concatenate(
+        side_products, axis=1
+    )
 
     global_rows = grid_index * middle_count + jnp.arange(middle_count, dtype=jnp.int32)
     global_columns = sibling_index * own_columns + jnp.arange(own_columns, dtype=jnp.int32)

time: 406 us -> 383 us (0.943)
  matrix products: 42.1 us -> 0 us
  Pallas kernels: 96.3 us -> 134 us
  waiting for transfers between devices: 175 us -> 148 us
  local copies, waits for them, and re-layouts: 29.1 us -> 39 us
    dot_general x4 -> x0, matrix products: 42.1 us -> none  [dot(): lax.dot_general(left, right, (((1,), (0,)), ((), ())), precision=near, pr...]
    pallas_call x0 -> x6, Pallas kernels: none -> 36.4 us  [the longest x2 31.5 us: mixed_times(): pl.pallas_call(functools.partial(mixed_kernel, len(left), len(left[0])),...]
    ppermute x41, waiting for transfers between devices: 175 us -> 147 us  [swap(): return lax.ppermute(value, axis, [(i, i ^ flip) for i in range(count)])]
    unnamed x74 -> x146, local copies, waits for them, and re-layouts: 8.06 us -> 30.8 us
    neg x0 -> x2, other arithmetic: none -> 10 us  [the longest x1 6.55 us: local(): -root_side]
    slice x8 -> x0, local copies, waits for them, and re-layouts: 7.64 us -> none  [the longest x6 5.51 us: transposed(): pair[count:]]
    slice x6, local copies, waits for them, and re-layouts: 10.6 us -> 5.66 us  [gather_chips(): onward = [held[0][:half], held[1][half:]]]
    concatenate x8 -> x0, other arithmetic: 4.54 us -> none  [the longest x6 3.41 us: transposed(): jnp.concatenate([columns_for(e), other_core[k * count:(k + 1) * count]],...]
  transfers between devices with their start and end apart: 42 -> 42, of which waited for: 18 -> 17; matrix products, arithmetic and copies ran while one was open for 14% -> 5% of each run, Pallas kernels for 21% -> 28%
where the time goes in v2:
time: 383 us
  waiting for transfers between devices  148 us (39%)
  Pallas kernels  134 us (35%)
  local copies, waits for them, and re-layouts  39 us (10%)
  starting transfers between devices  28.4 us (7%)
  other arithmetic  18.4 us (5%)
  between operations  14.8 us (4%)
    ppermute x41, waiting for transfers between devices, swap(): return lax.ppermute(value, axis, [(i, i ^ flip) for i in range(count)])  147 us
    pallas_call x4, Pallas kernels, root_times(): pl.pallas_call(functools.partial(root_kernel, count), grid_spec=pltpu.Pre...  62.3 us
    pallas_call x3, Pallas kernels, side_times(): pl.pallas_call(functools.partial(side_kernel, len(columns)), grid=(width...  35.1 us
    pallas_call x2, Pallas kernels, mixed_times(): pl.pallas_call(functools.partial(mixed_kernel, len(left), len(left[0])),...  31.5 us
    unnamed x146, local copies, waits for them, and re-layouts  30.8 us
    ppermute x41, starting transfers between devices, swap(): return lax.ppermute(value, axis, [(i, i ^ flip) for i in range(count)])  28.3 us
  transfers between devices with their start and end apart: 42, of which 17 were waited for; matrix products, arithmetic and copies ran while one was open for 5% of the time, Pallas kernels for 28%

profile of v2, /device:TPU:0, one launch (start us, length us, event | category | flops | bytes accessed | tf_op | source)
XLA Modules:
  0.0 382.5 jit_solution(18388710410764631284)
XLA Ops:
  8.8 2.9 collective-permute-start.1
  11.7 1.5 collective-permute-start.3
  14.1 2.5 broadcast_multiply_fusion
  16.6 1.8 fusion.4
  18.9 39.4 %collective-permute-done.1.refs_2_.refs_10_ = f32[512,1024]{1,0:T(8,128)} collective-permute-done((f32[512,1024]{1,0:T(8,128)S(1)}, f32[512,1024]{1,0:T(8,128)}, u32[]{:S(2)}, u32[]{:S(2)}) %collective-permute-start.1) | collective-permute-done | bytes 2097184 | tf_op jit(solution)/shard_map/ppermute | solution.py:226
  58.3 2.1 collective-permute-done.3.refs_4_.refs_12_
  60.4 1.3 slice.31
  61.7 1.6 collective-permute-start.5
  63.3 1.3 slice.32
  65.2 37.9 %collective-permute-done.9.refs_2_.refs_10_ = f32[512,1024]{1,0:T(8,128)S(1)} collective-permute-done((f32[512,1024]{1,0:T(8,128)S(1)}, f32[512,1024]{1,0:T(8,128)S(1)}, u32[]{:S(2)}, u32[]{:S(2)}) %collective-permute-start.9) | collective-permute-done | bytes 2097184 | tf_op jit(solution)/shard_map/ppermute | solution.py:226
  103.1 2.1 collective-permute-done.11.refs_4_.refs_12_
  105.4 1.6 collective-permute-start.14
  107.4 20.3 %collective-permute-done.5.refs_6_.refs_14_ = f32[256,1024]{1,0:T(8,128)S(1)} collective-permute-done((f32[256,1024]{1,0:T(8,128)S(1)}, f32[256,1024]{1,0:T(8,128)S(1)}, u32[]{:S(2)}, u32[]{:S(2)}) %collective-permute-start.5) | collective-permute-done | bytes 1048608 | tf_op jit(solution)/shard_map/ppermute | solution.py:226
  127.7 21.0 %collective-permute-done.14.refs_6_.refs_14_ = f32[256,1024]{1,0:T(8,128)S(1)} collective-permute-done((f32[256,1024]{1,0:T(8,128)S(1)}, f32[256,1024]{1,0:T(8,128)S(1)}, u32[]{:S(2)}, u32[]{:S(2)}) %collective-permute-start.14) | collective-permute-done | bytes 1048608 | tf_op jit(solution)/shard_map/ppermute | solution.py:226
  148.7 1.3 collective-permute-done.15.refs_7_.refs_15_
  151.5 1.1 copy-done.12
  152.7 1.0 copy-done.38
  155.4 1.0 copy-done.41
  157.8 1.7 collective-permute-start.21
  159.6 1.0 copy-done.44
  160.6 1.0 copy-done.47
  162.0 1.2 copy-done.9
  163.2 1.2 copy-done.13
  164.4 1.2 copy-done.17
  165.6 1.2 copy-done.21
  166.9 11.5 %shard_map.110.refs_0_ = f32[256,1024]{1,0:T(8,128)S(1)} custom-call(s32[1]{0:T(128)} %bitcast.index_ref, f32[512,4096]{1,0:T(8,128)} %all-gather.2.cloned.1.call-done.root_ref, f32[512,1024]{1,0:T(8,128)S(1)} %copy-done, f32[512,1024]{1,0:T(8,128)} %collective-permute-done.refs_1_.refs_9_, f32[512,1024]{1,0:T(8,128)} %collective-permute-done.1.refs_2_.refs_10_, ...), custom_call_target="tpu_custom_call" | custom-call | tf_op jit(solution)/shard_map/pallas_call | solution.py:139
  178.3 1.3 collective-permute-start.18
  179.7 1.2 copy-done.10
  181.0 1.2 copy-done.14
  182.2 1.2 copy-done.18
  183.4 1.2 copy-done.22
  184.6 11.4 %shard_map.111.refs_0_.refs_1_ = f32[256,1024]{1,0:T(8,128)S(1)} custom-call(s32[1]{0:T(128)} %bitcast.index_ref, f32[512,4096]{1,0:T(8,128)} %all-gather.2.cloned.1.call-done.root_ref, f32[512,1024]{1,0:T(8,128)S(1)} %copy-done, f32[512,1024]{1,0:T(8,128)} %collective-permute-done.refs_1_.refs_9_, f32[512,1024]{1,0:T(8,128)} %collective-permute-done.1.refs_2_.refs_10_, ...), custom_call_target="tpu_custom_call" | custom-call | tf_op jit(solution)/shard_map/pallas_call | solution.py:139
  196.1 9.6 %collective-permute-done.20.refs_2_.refs_10_ = f32[512,1024]{1,0:T(8,128)} collective-permute-done((f32[512,1024]{1,0:T(8,128)}, f32[512,1024]{1,0:T(8,128)}, u32[]{:S(2)}, u32[]{:S(2)}) %collective-permute-start.20) | collective-permute-done | bytes 2097184 | tf_op jit(solution)/shard_map/ppermute | solution.py:226
  205.8 1.7 shard_map.112
  207.6 1.8 collective-permute-start.23
  209.9 1.5 slice.36
  211.4 1.6 collective-permute-start.27
  213.0 1.3 slice.37
  214.3 1.6 collective-permute-start.28
  215.9 1.1 shard_map.113
  217.8 19.6 %shard_map.114 = f32[512,1024]{1,0:T(8,128)S(1)} custom-call(s32[1]{0:T(128)} %bitcast.index_ref, f32[512,4096]{1,0:T(8,128)} %all-gather.2.cloned.1.call-done.root_ref, f32[512,1024]{1,0:T(8,128)S(1)} %copy-done.3, f32[512,1024]{1,0:T(8,128)} %copy-done.66, f32[512,1024]{1,0:T(8,128)} %copy-done.64, f32[512,1024]{1,0:T(8,128)} %copy-done.67, ...), custom_call_target="tpu_custom_call" | custom-call | tf_op jit(solution)/shard_map/pallas_call | solution.py:139
  241.8 1.3 shard_map.116
  244.6 2.0 collective-permute-start.35
  246.6 1.0 copy-done.56
  250.1 5.7 %collective-permute-done.31.refs_2_ = f32[512,256]{1,0:T(8,128)S(1)} collective-permute-done((f32[512,256]{1,0:T(8,128)S(1)}, f32[512,256]{1,0:T(8,128)S(1)}, u32[]{:S(2)}, u32[]{:S(2)}) %collective-permute-start.31) | collective-permute-done | bytes 524320 | tf_op jit(solution)/shard_map/ppermute | solution.py:226
  257.5 1.2 copy-done.5
  258.7 1.2 copy-done.37
  260.0 18.4 %shard_map.117 = f32[512,2048]{1,0:T(8,128)S(1)} custom-call(s32[2]{0:T(128)S(1)} %pad_add_fusion.places_ref, f32[256,1024]{1,0:T(8,128)S(1)} %shard_map.110.refs_0_, f32[256,1024]{1,0:T(8,128)S(1)} %copy-done.5, f32[256,1024]{1,0:T(8,128)} %collective-permute-done.18.refs_1_.refs_2_, f32[256,1024]{1,0:T(8,128)S(1)} %copy-done.37, f32[2048,2048]{1,0:T(8,128)} %refs_3_.1, ...), custom_call_target="tpu_custom_call" | custom-call | tf_op jit(solution)/shard_map/pallas_call | solution.py:204
  278.4 2.0 copy-done.6
  280.5 19.8 %shard_map.118 = f32[512,1024]{1,0:T(8,128)S(1)} custom-call(s32[1]{0:T(128)} %bitcast.index_ref, f32[512,4096]{1,0:T(8,128)} %all-gather.2.cloned.1.call-done.root_ref, f32[512,1024]{1,0:T(8,128)} %get-tuple-element.56.refs_0_.refs_8_, f32[512,1024]{1,0:T(8,128)} %collective-permute-done.19.refs_1_.refs_9_, ...), custom_call_target="tpu_custom_call" | custom-call | tf_op jit(solution)/shard_map/pallas_call | solution.py:139
  300.3 1.3 copy-done.26
  301.7 11.6 %shard_map.119 = f32[256,1024]{1,0:T(8,128)S(1)} custom-call(f32[512,256]{1,0:T(8,128)S(1)} %copy-done.28, f32[512,256]{1,0:T(8,128)S(1)} %copy-done.34, f32[512,256]{1,0:T(8,128)S(1)} %copy-done.31, f32[512,256]{1,0:T(8,128)} %collective-permute-done.32.refs_3_, f32[512,256]{1,0:T(8,128)} %collective-permute-done.33.refs_4_, ...), custom_call_target="tpu_custom_call" | custom-call | tf_op jit(solution)/shard_map/pallas_call | solution.py:164
  313.4 1.2 select_reduce_fusion
  315.3 3.3 multiply_reduce_fusion.2
  319.1 6.5 %fusion.1 = (f32[512,2048]{1,0:T(8,128)}, f32[2048]{0:T(1024)S(1)}) fusion(f32[512,2048]{1,0:T(8,128)S(1)} %copy-done.7, f32[512,1024]{1,0:T(8,128)} %copy-done.26, f32[512,1024]{1,0:T(8,128)S(1)} %copy-done.25, f32[512,2048]{1,0:T(8,128)} %param.10, f32[512]{0:T(512)S(1)} %broadcast_bitcast_fusion), kind=kLoop, calls=%fused_computation.8 | loop fusion | flops 6289408 | bytes 16787456 | tf_op jit(solution)/shard_map/neg | solution.py:373
  325.7 11.9 %shard_map.121 = f32[256,1024]{1,0:T(8,128)S(1)} custom-call(f32[512,256]{1,0:T(8,128)S(1)} %copy-done.29, f32[512,256]{1,0:T(8,128)S(1)} %copy-done.35, f32[512,256]{1,0:T(8,128)S(1)} %copy-done.32, f32[512,256]{1,0:T(8,128)} %collective-permute-done.32.refs_3_, f32[512,256]{1,0:T(8,128)} %collective-permute-done.33.refs_4_, ...), custom_call_target="tpu_custom_call" | custom-call | tf_op jit(solution)/shard_map/pallas_call | solution.py:164
  337.7 11.5 %shard_map.120 = f32[256,1024]{1,0:T(8,128)S(1)} custom-call(f32[512,256]{1,0:T(8,128)S(1)} %copy-done.29, f32[512,256]{1,0:T(8,128)S(1)} %copy-done.35, f32[512,256]{1,0:T(8,128)S(1)} %copy-done.32, f32[512,256]{1,0:T(8,128)} %collective-permute-done.32.refs_3_, f32[512,256]{1,0:T(8,128)} %collective-permute-done.33.refs_4_, ...), custom_call_target="tpu_custom_call" | custom-call | tf_op jit(solution)/shard_map/pallas_call | solution.py:164
  349.3 13.1 %shard_map.122 = f32[256,2048]{1,0:T(8,128)S(1)} custom-call(s32[2]{0:T(128)S(1)} %pad_add_fusion.places_ref, f32[256,1024]{1,0:T(8,128)} %get-tuple-element.101.refs_0_, f32[256,1024]{1,0:T(8,128)} %collective-permute-done.37.refs_1_, f32[2048,2048]{1,0:T(8,128)} %refs_3_.1, f32[2048,2048]{1,0:T(8,128)} %refs_3_.1), custom_call_target="tpu_custom_call" | custom-call | tf_op jit(solution)/shard_map/pallas_call | solution.py:204
  362.4 3.5 fusion.2
  365.9 1.2 collective-permute-done.38
  367.1 1.4 collective-permute-start.39
  368.5 2.3 collective-permute-done.39
  370.8 1.4 collective-permute-start.40
  372.1 2.3 collective-permute-done.40
  (206 shorter events, 23.3 us)
Async XLA Ops:
  7.2 154.8 %all-gather.2.cloned.1.call-start = ((), (), s32[]{:S(2)}) async-start(), calls=%async_computation | async-start | bytes 10485760 | tf_op jit(solution)/shard_map/all_gather | solution.py:290
  8.8 49.5 %collective-permute-start.1 = (f32[512,1024]{1,0:T(8,128)S(1)}, f32[512,1024]{1,0:T(8,128)}, u32[]{:S(2)}, u32[]{:S(2)}) collective-permute-start(f32[512,1024]{1,0:T(8,128)S(1)} %copy-done), channel_id=1, source_target_pairs={{0,2},{1,3},{2,0},{3,1},{4,6},{5,7},{6,4},{7,5},{8,10},{9,11},{10,... | collective-permute-start | bytes 6291464 | tf_op jit(solution)/shard_map/ppermute | solution.py:226
  11.7 48.7 %collective-permute-start.3 = (f32[512,1024]{1,0:T(8,128)S(1)}, f32[512,1024]{1,0:T(8,128)}, u32[]{:S(2)}, u32[]{:S(2)}) collective-permute-start(f32[512,1024]{1,0:T(8,128)S(1)} %copy-done), channel_id=1, source_target_pairs={{0,4},{1,5},{2,6},{3,7},{4,0},{5,1},{6,2},{7,3},{8,12},{9,13},{10,... | collective-permute-start | bytes 6291464 | tf_op jit(solution)/shard_map/ppermute | solution.py:226
  13.2 47.1 %collective-permute-start = (f32[512,1024]{1,0:T(8,128)S(1)}, f32[512,1024]{1,0:T(8,128)}, u32[]{:S(2)}, u32[]{:S(2)}) collective-permute-start(f32[512,1024]{1,0:T(8,128)S(1)} %copy-done), channel_id=1, source_target_pairs={{0,1},{1,0},{2,3},{3,2},{4,5},{5,4},{6,7},{7,6},{8,9},{9,8},{10,11... | collective-permute-start | bytes 6291464 | tf_op jit(solution)/shard_map/ppermute | solution.py:226
  18.3 46.3 %copy-start.2 = (f32[512,1024]{1,0:T(8,128)}, f32[512,1024]{1,0:T(8,128)S(1)}, u32[]{:S(2)}) copy-start(f32[512,1024]{1,0:T(8,128)S(1)} %get-tuple-element.107.refs_0_.refs_8_) | copy-start | bytes 6291460
  18.4 84.7 %collective-permute-start.9 = (f32[512,1024]{1,0:T(8,128)S(1)}, f32[512,1024]{1,0:T(8,128)S(1)}, u32[]{:S(2)}, u32[]{:S(2)}) collective-permute-start(f32[512,1024]{1,0:T(8,128)S(1)} %get-tuple-element.107.refs_0_.refs_8_), channel_id=1, source_target_pairs={{0,2},{1,3},{2,0},{3,1},{4,6},{5,7},{6,4},{7,5},{8,10},{9,11},{10,... | collective-permute-start | bytes 6291464 | tf_op jit(solution)/shard_map/ppermute | solution.py:226
  18.9 86.3 %collective-permute-start.11 = (f32[512,1024]{1,0:T(8,128)S(1)}, f32[512,1024]{1,0:T(8,128)S(1)}, u32[]{:S(2)}, u32[]{:S(2)}) collective-permute-start(f32[512,1024]{1,0:T(8,128)S(1)} %get-tuple-element.107.refs_0_.refs_8_), channel_id=1, source_target_pairs={{0,4},{1,5},{2,6},{3,7},{4,0},{5,1},{6,2},{7,3},{8,12},{9,13},{10,... | collective-permute-start | bytes 6291464 | tf_op jit(solution)/shard_map/ppermute | solution.py:226
  58.3 46.9 %collective-permute-start.13 = (f32[512,1024]{1,0:T(8,128)S(1)}, f32[512,1024]{1,0:T(8,128)S(1)}, u32[]{:S(2)}, u32[]{:S(2)}) collective-permute-start(f32[512,1024]{1,0:T(8,128)S(1)} %get-tuple-element.107.refs_0_.refs_8_), channel_id=1, source_target_pairs={{0,1},{1,0},{2,3},{3,2},{4,5},{5,4},{6,7},{7,6},{8,9},{9,8},{10,11... | collective-permute-start | bytes 6291464 | tf_op jit(solution)/shard_map/ppermute | solution.py:226
  61.7 66.0 %collective-permute-start.5 = (f32[256,1024]{1,0:T(8,128)S(1)}, f32[256,1024]{1,0:T(8,128)S(1)}, u32[]{:S(2)}, u32[]{:S(2)}) collective-permute-start(f32[256,1024]{1,0:T(8,128)S(1)} %slice.31), channel_id=1, source_target_pairs={{0,4},{1,5},{2,6},{3,7},{4,0},{5,1},{6,2},{7,3},{8,12},{9,13},{10,... | collective-permute-start | bytes 3145736 | tf_op jit(solution)/shard_map/ppermute | solution.py:226
  64.6 63.0 %collective-permute-start.6 = (f32[256,1024]{1,0:T(8,128)S(1)}, f32[256,1024]{1,0:T(8,128)S(1)}, u32[]{:S(2)}, u32[]{:S(2)}) collective-permute-start(f32[256,1024]{1,0:T(8,128)S(1)} %slice.32), channel_id=1, source_target_pairs={{0,2},{1,3},{2,0},{3,1},{4,6},{5,7},{6,4},{7,5},{8,10},{9,11},{10,... | collective-permute-start | bytes 3145736 | tf_op jit(solution)/shard_map/ppermute | solution.py:226
  105.2 54.4 %copy-start.66 = (f32[512,1024]{1,0:T(8,128)}, f32[512,1024]{1,0:T(8,128)S(1)}, u32[]{:S(2)}) copy-start(f32[512,1024]{1,0:T(8,128)S(1)} %collective-permute-done.13.refs_1_.refs_9_) | copy-start | bytes 6291460
  105.2 45.8 %collective-permute-start.10 = (f32[512,1024]{1,0:T(8,128)S(1)}, f32[512,1024]{1,0:T(8,128)S(1)}, u32[]{:S(2)}, u32[]{:S(2)}) collective-permute-start(f32[512,1024]{1,0:T(8,128)S(1)} %collective-permute-done.9.refs_2_.refs_10_), channel_id=1, source_target_pairs={{0,1},{1,0},{2,3},{3,2},{4,5},{5,4},{6,7},{7,6},{8,9},{9,8},{10,11... | collective-permute-start | bytes 6291464 | tf_op jit(solution)/shard_map/ppermute | solution.py:226
  105.4 43.3 %collective-permute-start.14 = (f32[256,1024]{1,0:T(8,128)S(1)}, f32[256,1024]{1,0:T(8,128)S(1)}, u32[]{:S(2)}, u32[]{:S(2)}) collective-permute-start(f32[256,1024]{1,0:T(8,128)S(1)} %slice.34), channel_id=1, source_target_pairs={{0,4},{1,5},{2,6},{3,7},{4,0},{5,1},{6,2},{7,3},{8,12},{9,13},{10,... | collective-permute-start | bytes 3145736 | tf_op jit(solution)/shard_map/ppermute | solution.py:226
  107.1 45.5 %collective-permute-start.12 = (f32[512,1024]{1,0:T(8,128)S(1)}, f32[512,1024]{1,0:T(8,128)S(1)}, u32[]{:S(2)}, u32[]{:S(2)}) collective-permute-start(f32[512,1024]{1,0:T(8,128)S(1)} %collective-permute-done.11.refs_4_.refs_12_), channel_id=1, source_target_pairs={{0,1},{1,0},{2,3},{3,2},{4,5},{5,4},{6,7},{7,6},{8,9},{9,8},{10,11... | collective-permute-start | bytes 6291464 | tf_op jit(solution)/shard_map/ppermute | solution.py:226
  127.7 22.3 %collective-permute-start.15 = (f32[256,1024]{1,0:T(8,128)S(1)}, f32[256,1024]{1,0:T(8,128)S(1)}, u32[]{:S(2)}, u32[]{:S(2)}) collective-permute-start(f32[256,1024]{1,0:T(8,128)S(1)} %slice.35), channel_id=1, source_target_pairs={{0,2},{1,3},{2,0},{3,1},{4,6},{5,7},{6,4},{7,5},{8,10},{9,11},{10,... | collective-permute-start | bytes 3145736 | tf_op jit(solution)/shard_map/ppermute | solution.py:226
  127.7 29.7 %collective-permute-start.2 = (f32[512,1024]{1,0:T(8,128)}, f32[512,1024]{1,0:T(8,128)S(1)}, u32[]{:S(2)}, u32[]{:S(2)}) collective-permute-start(f32[512,1024]{1,0:T(8,128)} %collective-permute-done.1.refs_2_.refs_10_), channel_id=1, source_target_pairs={{0,1},{1,0},{2,3},{3,2},{4,5},{5,4},{6,7},{7,6},{8,9},{9,8},{10,11... | collective-permute-start | bytes 6291464 | tf_op jit(solution)/shard_map/ppermute | solution.py:226
  148.7 8.7 %collective-permute-start.4 = (f32[512,1024]{1,0:T(8,128)}, f32[512,1024]{1,0:T(8,128)S(1)}, u32[]{:S(2)}, u32[]{:S(2)}) collective-permute-start(f32[512,1024]{1,0:T(8,128)} %collective-permute-done.3.refs_4_.refs_12_), channel_id=1, source_target_pairs={{0,1},{1,0},{2,3},{3,2},{4,5},{5,4},{6,7},{7,6},{8,9},{9,8},{10,11... | collective-permute-start | bytes 6291464 | tf_op jit(solution)/shard_map/ppermute | solution.py:226
  150.0 4.3 %collective-permute-start.7 = (f32[256,1024]{1,0:T(8,128)S(1)}, f32[256,1024]{1,0:T(8,128)S(1)}, u32[]{:S(2)}, u32[]{:S(2)}) collective-permute-start(f32[256,1024]{1,0:T(8,128)S(1)} %collective-permute-done.5.refs_6_.refs_14_), channel_id=1, source_target_pairs={{0,1},{1,0},{2,3},{3,2},{4,5},{5,4},{6,7},{7,6},{8,9},{9,8},{10,11... | collective-permute-start | bytes 3145736 | tf_op jit(solution)/shard_map/ppermute | solution.py:226
  151.0 5.4 %collective-permute-start.8 = (f32[256,1024]{1,0:T(8,128)S(1)}, f32[256,1024]{1,0:T(8,128)S(1)}, u32[]{:S(2)}, u32[]{:S(2)}) collective-permute-start(f32[256,1024]{1,0:T(8,128)S(1)} %collective-permute-done.6.refs_7_.refs_15_), channel_id=1, source_target_pairs={{0,1},{1,0},{2,3},{3,2},{4,5},{5,4},{6,7},{7,6},{8,9},{9,8},{10,11... | collective-permute-start | bytes 3145736 | tf_op jit(solution)/shard_map/ppermute | solution.py:226
  152.6 6.9 %collective-permute-start.16 = (f32[256,1024]{1,0:T(8,128)S(1)}, f32[256,1024]{1,0:T(8,128)S(1)}, u32[]{:S(2)}, u32[]{:S(2)}) collective-permute-start(f32[256,1024]{1,0:T(8,128)S(1)} %collective-permute-done.14.refs_6_.refs_14_), channel_id=1, source_target_pairs={{0,1},{1,0},{2,3},{3,2},{4,5},{5,4},{6,7},{7,6},{8,9},{9,8},{10,11... | collective-permute-start | bytes 3145736 | tf_op jit(solution)/shard_map/ppermute | solution.py:226
  155.3 5.3 %collective-permute-start.17 = (f32[256,1024]{1,0:T(8,128)S(1)}, f32[256,1024]{1,0:T(8,128)S(1)}, u32[]{:S(2)}, u32[]{:S(2)}) collective-permute-start(f32[256,1024]{1,0:T(8,128)S(1)} %collective-permute-done.15.refs_7_.refs_15_), channel_id=1, source_target_pairs={{0,1},{1,0},{2,3},{3,2},{4,5},{5,4},{6,7},{7,6},{8,9},{9,8},{10,11... | collective-permute-start | bytes 3145736 | tf_op jit(solution)/shard_map/ppermute | solution.py:226
  157.4 48.3 %collective-permute-start.20 = (f32[512,1024]{1,0:T(8,128)}, f32[512,1024]{1,0:T(8,128)}, u32[]{:S(2)}, u32[]{:S(2)}) collective-permute-start(f32[512,1024]{1,0:T(8,128)} %get-tuple-element.56.refs_0_.refs_8_), channel_id=1, source_target_pairs={{0,2},{1,3},{2,0},{3,1},{4,6},{5,7},{6,4},{7,5},{8,10},{9,11},{10,... | collective-permute-start | bytes 6291464 | tf_op jit(solution)/shard_map/ppermute | solution.py:226
  157.8 48.0 %collective-permute-start.21 = (f32[512,1024]{1,0:T(8,128)}, f32[512,1024]{1,0:T(8,128)}, u32[]{:S(2)}, u32[]{:S(2)}) collective-permute-start(f32[512,1024]{1,0:T(8,128)} %get-tuple-element.56.refs_0_.refs_8_), channel_id=1, source_target_pairs={{0,4},{1,5},{2,6},{3,7},{4,0},{5,1},{6,2},{7,3},{8,12},{9,13},{10,... | collective-permute-start | bytes 6291464 | tf_op jit(solution)/shard_map/ppermute | solution.py:226
  159.5 46.3 %collective-permute-start.19 = (f32[512,1024]{1,0:T(8,128)}, f32[512,1024]{1,0:T(8,128)}, u32[]{:S(2)}, u32[]{:S(2)}) collective-permute-start(f32[512,1024]{1,0:T(8,128)} %get-tuple-element.56.refs_0_.refs_8_), channel_id=1, source_target_pairs={{0,1},{1,0},{2,3},{3,2},{4,5},{5,4},{6,7},{7,6},{8,9},{9,8},{10,11... | collective-permute-start | bytes 6291464 | tf_op jit(solution)/shard_map/ppermute | solution.py:226
  178.3 27.5 %collective-permute-start.18 = (f32[256,1024]{1,0:T(8,128)S(1)}, f32[256,1024]{1,0:T(8,128)}, u32[]{:S(2)}, u32[]{:S(2)}) collective-permute-start(f32[256,1024]{1,0:T(8,128)S(1)} %shard_map.110.refs_0_), channel_id=1, source_target_pairs={{0,8},{8,0},{16,24},{24,16},{1,9},{9,1},{17,25},{25,17},{2,10},{10... | collective-permute-start | bytes 3145736 | tf_op jit(solution)/shard_map/ppermute | solution.py:226
  196.1 41.4 %copy-start.4 = (f32[256,1024]{1,0:T(8,128)}, f32[256,1024]{1,0:T(8,128)S(1)}, u32[]{:S(2)}) copy-start(f32[256,1024]{1,0:T(8,128)S(1)} %shard_map.111.refs_0_.refs_1_) | copy-start | bytes 3145732
  207.5 6.8 %collective-permute-start.22 = (f32[1024,256]{1,0:T(8,128)S(1)}, f32[1024,256]{1,0:T(8,128)S(1)}, u32[]{:S(2)}, u32[]{:S(2)}) collective-permute-start(f32[1024,256]{1,0:T(8,128)S(1)} %get-tuple-element.64), channel_id=1, source_target_pairs={{0,1},{1,0},{2,3},{3,2},{4,5},{5,4},{6,7},{7,6},{8,9},{9,8},{10,11... | collective-permute-start | bytes 3145736 | tf_op jit(solution)/shard_map/ppermute | solution.py:226
  207.6 29.9 %collective-permute-start.23 = (f32[256,1024]{1,0:T(8,128)S(1)}, f32[256,1024]{1,0:T(8,128)S(1)}, u32[]{:S(2)}, u32[]{:S(2)}) collective-permute-start(f32[256,1024]{1,0:T(8,128)S(1)} %shard_map.111.refs_0_.refs_1_), channel_id=1, source_target_pairs={{0,8},{8,0},{16,24},{24,16},{1,9},{9,1},{17,25},{25,17},{2,10},{10... | collective-permute-start | bytes 3145736 | tf_op jit(solution)/shard_map/ppermute | solution.py:226
  209.4 34.5 %collective-permute-start.25 = (f32[512,1024]{1,0:T(8,128)}, f32[512,1024]{1,0:T(8,128)S(1)}, u32[]{:S(2)}, u32[]{:S(2)}) collective-permute-start(f32[512,1024]{1,0:T(8,128)} %collective-permute-done.20.refs_2_.refs_10_), channel_id=1, source_target_pairs={{0,1},{1,0},{2,3},{3,2},{4,5},{5,4},{6,7},{7,6},{8,9},{9,8},{10,11... | collective-permute-start | bytes 6291464 | tf_op jit(solution)/shard_map/ppermute | solution.py:226
  209.5 35.0 %collective-permute-start.26 = (f32[512,1024]{1,0:T(8,128)}, f32[512,1024]{1,0:T(8,128)S(1)}, u32[]{:S(2)}, u32[]{:S(2)}) collective-permute-start(f32[512,1024]{1,0:T(8,128)} %collective-permute-done.21.refs_4_.refs_12_), channel_id=1, source_target_pairs={{0,1},{1,0},{2,3},{3,2},{4,5},{5,4},{6,7},{7,6},{8,9},{9,8},{10,11... | collective-permute-start | bytes 6291464 | tf_op jit(solution)/shard_map/ppermute | solution.py:226
  211.4 27.0 %collective-permute-start.27 = (f32[256,1024]{1,0:T(8,128)S(1)}, f32[256,1024]{1,0:T(8,128)S(1)}, u32[]{:S(2)}, u32[]{:S(2)}) collective-permute-start(f32[256,1024]{1,0:T(8,128)S(1)} %slice.36), channel_id=1, source_target_pairs={{0,4},{1,5},{2,6},{3,7},{4,0},{5,1},{6,2},{7,3},{8,12},{9,13},{10,... | collective-permute-start | bytes 3145736 | tf_op jit(solution)/shard_map/ppermute | solution.py:226
  214.3 25.0 %collective-permute-start.28 = (f32[256,1024]{1,0:T(8,128)S(1)}, f32[256,1024]{1,0:T(8,128)S(1)}, u32[]{:S(2)}, u32[]{:S(2)}) collective-permute-start(f32[256,1024]{1,0:T(8,128)S(1)} %slice.37), channel_id=1, source_target_pairs={{0,2},{1,3},{2,0},{3,1},{4,6},{5,7},{6,4},{7,5},{8,10},{9,11},{10,... | collective-permute-start | bytes 3145736 | tf_op jit(solution)/shard_map/ppermute | solution.py:226
  238.3 2.7 collective-permute-start.24
  238.4 17.4 %copy-start.50 = (f32[256,1024]{1,0:T(8,128)}, f32[256,1024]{1,0:T(8,128)S(1)}, u32[]{:S(2)}) copy-start(f32[256,1024]{1,0:T(8,128)S(1)} %collective-permute-done.27.refs_6_.refs_14_) | copy-start | bytes 3145732
  238.4 8.2 %collective-permute-start.29 = (f32[256,1024]{1,0:T(8,128)S(1)}, f32[256,1024]{1,0:T(8,128)S(1)}, u32[]{:S(2)}, u32[]{:S(2)}) collective-permute-start(f32[256,1024]{1,0:T(8,128)S(1)} %collective-permute-done.27.refs_6_.refs_14_), channel_id=1, source_target_pairs={{0,1},{1,0},{2,3},{3,2},{4,5},{5,4},{6,7},{7,6},{8,9},{9,8},{10,11... | collective-permute-start | bytes 3145736 | tf_op jit(solution)/shard_map/ppermute | solution.py:226
  239.3 9.1 %collective-permute-start.30 = (f32[256,1024]{1,0:T(8,128)S(1)}, f32[256,1024]{1,0:T(8,128)S(1)}, u32[]{:S(2)}, u32[]{:S(2)}) collective-permute-start(f32[256,1024]{1,0:T(8,128)S(1)} %collective-permute-done.28.refs_7_.refs_15_), channel_id=1, source_target_pairs={{0,1},{1,0},{2,3},{3,2},{4,5},{5,4},{6,7},{7,6},{8,9},{9,8},{10,11... | collective-permute-start | bytes 3145736 | tf_op jit(solution)/shard_map/ppermute | solution.py:226
  241.0 14.8 %collective-permute-start.31 = (f32[512,256]{1,0:T(8,128)S(1)}, f32[512,256]{1,0:T(8,128)S(1)}, u32[]{:S(2)}, u32[]{:S(2)}) collective-permute-start(f32[512,256]{1,0:T(8,128)S(1)} %get-tuple-element.66), channel_id=1, source_target_pairs={{0,2},{1,3},{2,0},{3,1},{4,6},{5,7},{6,4},{7,5},{8,10},{9,11},{10,... | collective-permute-start | bytes 1572872 | tf_op jit(solution)/shard_map/ppermute | solution.py:226
  243.9 12.7 %copy-start.69 = (f32[512,1024]{1,0:T(8,128)}, f32[512,1024]{1,0:T(8,128)S(1)}, u32[]{:S(2)}) copy-start(f32[512,1024]{1,0:T(8,128)S(1)} %collective-permute-done.25.refs_3_.refs_11_) | copy-start | bytes 6291460
  243.9 57.7 %collective-permute-start.33 = (f32[512,256]{1,0:T(8,128)}, f32[512,256]{1,0:T(8,128)}, u32[]{:S(2)}, u32[]{:S(2)}) collective-permute-start(f32[512,256]{1,0:T(8,128)} %get-tuple-element.67), channel_id=1, source_target_pairs={{0,4},{1,5},{2,6},{3,7},{4,0},{5,1},{6,2},{7,3},{8,12},{9,13},{10,... | collective-permute-start | bytes 1572872 | tf_op jit(solution)/shard_map/ppermute | solution.py:226
  244.6 12.0 %copy-start.70 = (f32[512,1024]{1,0:T(8,128)}, f32[512,1024]{1,0:T(8,128)S(1)}, u32[]{:S(2)}) copy-start(f32[512,1024]{1,0:T(8,128)S(1)} %collective-permute-done.26.refs_5_.refs_13_) | copy-start | bytes 6291460
  244.6 57.1 %collective-permute-start.35 = (f32[512,256]{1,0:T(8,128)}, f32[512,256]{1,0:T(8,128)}, u32[]{:S(2)}, u32[]{:S(2)}) collective-permute-start(f32[512,256]{1,0:T(8,128)} %get-tuple-element.68), channel_id=1, source_target_pairs={{0,6},{1,7},{2,4},{3,5},{4,2},{5,3},{6,0},{7,1},{8,14},{9,15},{10,... | collective-permute-start | bytes 1572872 | tf_op jit(solution)/shard_map/ppermute | solution.py:226
  247.6 54.0 %collective-permute-start.32 = (f32[512,256]{1,0:T(8,128)}, f32[512,256]{1,0:T(8,128)}, u32[]{:S(2)}, u32[]{:S(2)}) collective-permute-start(f32[512,256]{1,0:T(8,128)} %get-tuple-element.75), channel_id=1, source_target_pairs={{0,2},{1,3},{2,0},{3,1},{4,6},{5,7},{6,4},{7,5},{8,10},{9,11},{10,... | collective-permute-start | bytes 1572872 | tf_op jit(solution)/shard_map/ppermute | solution.py:226
  249.4 52.3 %collective-permute-start.34 = (f32[512,256]{1,0:T(8,128)}, f32[512,256]{1,0:T(8,128)}, u32[]{:S(2)}, u32[]{:S(2)}) collective-permute-start(f32[512,256]{1,0:T(8,128)} %get-tuple-element.76), channel_id=1, source_target_pairs={{0,4},{1,5},{2,6},{3,7},{4,0},{5,1},{6,2},{7,3},{8,12},{9,13},{10,... | collective-permute-start | bytes 1572872 | tf_op jit(solution)/shard_map/ppermute | solution.py:226
  256.6 45.1 %collective-permute-start.36 = (f32[512,256]{1,0:T(8,128)}, f32[512,256]{1,0:T(8,128)}, u32[]{:S(2)}, u32[]{:S(2)}) collective-permute-start(f32[512,256]{1,0:T(8,128)} %get-tuple-element.77), channel_id=1, source_target_pairs={{0,6},{1,7},{2,4},{3,5},{4,2},{5,3},{6,0},{7,1},{8,14},{9,15},{10,... | collective-permute-start | bytes 1572872 | tf_op jit(solution)/shard_map/ppermute | solution.py:226
  260.0 20.5 %copy-start.51 = (f32[256,1024]{1,0:T(8,128)S(1)}, f32[256,1024]{1,0:T(8,128)}, u32[]{:S(2)}) copy-start(f32[256,1024]{1,0:T(8,128)} %copy-done.50) | copy-start | bytes 3145732
  260.0 20.5 %copy-start.54 = (f32[256,1024]{1,0:T(8,128)S(1)}, f32[256,1024]{1,0:T(8,128)}, u32[]{:S(2)}) copy-start(f32[256,1024]{1,0:T(8,128)} %copy-done.53) | copy-start | bytes 3145732
  260.0 20.5 %copy-start.57 = (f32[256,1024]{1,0:T(8,128)S(1)}, f32[256,1024]{1,0:T(8,128)}, u32[]{:S(2)}) copy-start(f32[256,1024]{1,0:T(8,128)} %copy-done.56) | copy-start | bytes 3145732
  260.0 20.5 %copy-start.60 = (f32[256,1024]{1,0:T(8,128)S(1)}, f32[256,1024]{1,0:T(8,128)}, u32[]{:S(2)}) copy-start(f32[256,1024]{1,0:T(8,128)} %copy-done.59) | copy-start | bytes 3145732
  280.5 21.2 %copy-start.11 = (f32[256,1024]{1,0:T(8,128)S(1)}, f32[256,1024]{1,0:T(8,128)}, u32[]{:S(2)}) copy-start(f32[256,1024]{1,0:T(8,128)} %copy-done.8) | copy-start | bytes 3145732
  280.5 21.2 %copy-start.15 = (f32[256,1024]{1,0:T(8,128)S(1)}, f32[256,1024]{1,0:T(8,128)}, u32[]{:S(2)}) copy-start(f32[256,1024]{1,0:T(8,128)} %copy-done.12) | copy-start | bytes 3145732
  280.5 21.2 %copy-start.19 = (f32[256,1024]{1,0:T(8,128)S(1)}, f32[256,1024]{1,0:T(8,128)}, u32[]{:S(2)}) copy-start(f32[256,1024]{1,0:T(8,128)} %copy-done.16) | copy-start | bytes 3145732
  280.5 21.2 %copy-start.23 = (f32[256,1024]{1,0:T(8,128)S(1)}, f32[256,1024]{1,0:T(8,128)}, u32[]{:S(2)}) copy-start(f32[256,1024]{1,0:T(8,128)} %copy-done.20) | copy-start | bytes 3145732
  280.5 21.2 %copy-start.28 = (f32[512,256]{1,0:T(8,128)S(1)}, f32[512,256]{1,0:T(8,128)}, u32[]{:S(2)}) copy-start(f32[512,256]{1,0:T(8,128)} %copy-done.27) | copy-start | bytes 1572868
  280.5 21.2 %copy-start.31 = (f32[512,256]{1,0:T(8,128)S(1)}, f32[512,256]{1,0:T(8,128)}, u32[]{:S(2)}) copy-start(f32[512,256]{1,0:T(8,128)} %copy-done.30) | copy-start | bytes 1572868
  280.5 21.2 %copy-start.34 = (f32[512,256]{1,0:T(8,128)S(1)}, f32[512,256]{1,0:T(8,128)}, u32[]{:S(2)}) copy-start(f32[512,256]{1,0:T(8,128)} %copy-done.33) | copy-start | bytes 1572868
  314.5 34.8 %collective-permute-start.37 = (f32[256,1024]{1,0:T(8,128)}, f32[256,1024]{1,0:T(8,128)}, u32[]{:S(2)}, u32[]{:S(2)}) collective-permute-start(f32[256,1024]{1,0:T(8,128)} %get-tuple-element.101.refs_0_), channel_id=1, source_target_pairs={{0,8},{8,0},{16,24},{24,16},{1,9},{9,1},{17,25},{25,17},{2,10},{10... | collective-permute-start | bytes 3145736 | tf_op jit(solution)/shard_map/ppermute | solution.py:226
  325.7 12.0 %copy-start.40 = (f32[256,1024]{1,0:T(8,128)S(1)}, f32[256,1024]{1,0:T(8,128)}, u32[]{:S(2)}) copy-start(f32[256,1024]{1,0:T(8,128)} %copy-done.38) | copy-start | bytes 3145732
  325.7 12.0 %copy-start.43 = (f32[256,1024]{1,0:T(8,128)S(1)}, f32[256,1024]{1,0:T(8,128)}, u32[]{:S(2)}) copy-start(f32[256,1024]{1,0:T(8,128)} %copy-done.41) | copy-start | bytes 3145732
  325.7 12.0 %copy-start.46 = (f32[256,1024]{1,0:T(8,128)S(1)}, f32[256,1024]{1,0:T(8,128)}, u32[]{:S(2)}) copy-start(f32[256,1024]{1,0:T(8,128)} %copy-done.44) | copy-start | bytes 3145732
  325.7 12.0 %copy-start.49 = (f32[256,1024]{1,0:T(8,128)S(1)}, f32[256,1024]{1,0:T(8,128)}, u32[]{:S(2)}) copy-start(f32[256,1024]{1,0:T(8,128)} %copy-done.47) | copy-start | bytes 3145732
  362.4 12.7 %copy-start.72 = (f32[2048]{0:T(1024)S(1)}, f32[2048]{0:T(1024)}, u32[]{:S(2)}) copy-start(f32[2048]{0:T(1024)} %param.13) | copy-start | bytes 24580
  365.9 1.2 collective-permute-start.38
  367.1 3.7 collective-permute-start.39
  370.8 3.7 collective-permute-start.40
  (51 other events, 169.6 us)
Sparse Core Ops, SparseCore 0:
  9.6 152.3 all-gather.1

commit v3 on v2

--- a/solution.py
+++ b/solution.py
@@ -175,7 +175,8 @@
 
 
 def mixed_kernel(parts, pieces, places_ref, *refs):
-    left_refs, right_refs, out_ref = refs[: parts * pieces], refs[parts * pieces : -5], refs[-5]
+    left_refs, refs = refs[: parts * pieces], refs[parts * pieces :]
+    right_refs, refs = refs[:parts], refs[parts:]
     left_high, left_low, high, low = refs[-4:]
 
     @pl.when(pl.program_id(0) == 0)
@@ -189,14 +190,43 @@
                 top += count
 
     split_blocks(right_refs, high, low)
-    out_ref[...] = split_dot(left_high[...], left_low[...], high[...], low[...])
-
-
-def mixed_times(places, left, right):
+    product = split_dot(left_high[...], left_low[...], high[...], low[...])
+    if len(refs) == 5:
+        refs[0][...] = product
+        return
+    side_refs, (rows_ref, out_ref, sums_ref) = refs[:-7], refs[-7:-4]
+    for c, side_ref in enumerate(side_refs):
+
+        @pl.when(pl.program_id(0) // (pl.num_programs(0) // len(side_refs)) == c)
+        def _():
+            negative = side_ref[...] - product
+            out_ref[...] = negative
+            sums_ref[...] = -jnp.sum(rows_ref[...] * negative, axis=0, keepdims=True)
+
+
+def mixed_times(places, left, right, sides=()):
     height = sum(piece.shape[0] for piece in left[0])
     own = left[0][0].shape[1]
     depth, width = right.shape
     tile = min(width, 256)
+    out_specs = [pl.BlockSpec((height, tile), lambda i, p: (0, i))]
+    out_shape = [jax.ShapeDtypeStruct((height, width), jnp.float32)]
+    extra, extra_specs = [], []
+    if sides:
+        tiles = width // tile // len(sides)
+
+        def part(c):
+            def place(i, places):
+                return 0, jnp.clip(i - c * tiles, 0, tiles - 1)
+
+            return pl.BlockSpec((height, tile), place)
+
+        extra = [*sides, right]
+        extra_specs = [part(c) for c in range(len(sides))] + [
+            pl.BlockSpec((height, tile), lambda i, places: (places[len(left)], i))
+        ]
+        out_specs = out_specs + [pl.BlockSpec((1, tile), lambda i, p: (0, i))]
+        out_shape = out_shape + [jax.ShapeDtypeStruct((1, width), jnp.float32)]
 
     def band(s):
         return pl.BlockSpec((own, tile), lambda i, places: (places[s], i))
@@ -207,14 +237,15 @@
             num_scalar_prefetch=1,
             grid=(width // tile,),
             in_specs=[whole_spec(piece, lambda i, p: (0, 0)) for part in left for piece in part]
-            + [band(s) for s in range(len(left))],
-            out_specs=pl.BlockSpec((height, tile), lambda i, p: (0, i)),
+            + [band(s) for s in range(len(left))]
+            + extra_specs,
+            out_specs=out_specs,
             scratch_shapes=panel_scratch(height, depth, tile),
         ),
-        out_shape=jax.ShapeDtypeStruct((height, width), jnp.float32),
+        out_shape=out_shape,
         compiler_params=pltpu.CompilerParams(vmem_limit_bytes=44 * 2**20),
         cost_estimate=unhidden,
-    )(places, *[piece for part in left for piece in part], *[right] * len(left))
+    )(places, *[piece for part in left for piece in part], *[right] * len(left), *extra)
 
 
 def after(value, other):
@@ -279,7 +310,8 @@
     chunk = min(width, 1024)
     chunks = range(width // chunk)
 
-    places = jnp.stack([sibling_index ^ s for s in range(siblings)]).astype(jnp.int32)
+    places = [sibling_index ^ s for s in range(siblings)] + [grid_index]
+    places = jnp.stack(places).astype(jnp.int32)
 
     blocks_here = local_rows // BLK
     pattern = lax.dynamic_slice(
@@ -328,15 +360,22 @@
     sent = [
         [half] + [swap(half, "leaf", s) for s in range(1, siblings)] for half in first_halves
     ]
-    sent[0] = after(sent[0], arrived)
+    global_rows = grid_index * middle_count + jnp.arange(middle_count, dtype=jnp.int32)
+    global_columns = sibling_index * own_columns + jnp.arange(own_columns, dtype=jnp.int32)
+    on_diagonal = global_rows[:, None] == global_columns[None, :]
+    first_side = jnp.concatenate(first_halves, axis=0)
+    middle_cross = -first_side
+    middle_part = jnp.sum(jnp.where(on_diagonal, middle_inverse, 0.0), axis=0) + jnp.sum(
+        middle_panel * first_side, axis=0
+    )
+    sent[0] = after(sent[0], (arrived, middle_cross, middle_part))
     outgoing, upper_columns = transposed(sent[0])
     ready = after(root_rows, outgoing)
     root_sides = [root_times(index, ready, lower_blocks[0])]
     sent[1] = after(sent[1], root_sides)
     outgoing, lower_columns = transposed(sent[1])
-    first_side = jnp.concatenate(first_halves, axis=0)
     left = [[sent[0][s], sent[1][s]] for s in range(siblings)]
-    mixed = mixed_times(places, after(left, outgoing), lower_middle)
+    (mixed,) = mixed_times(places, after(left, outgoing), lower_middle)
     ready = after(root_rows, mixed)
     root_sides += [root_times(index, ready, blocks) for blocks in lower_blocks[1:]]
     root_side = jnp.concatenate(root_sides, axis=1) - mixed
@@ -348,20 +387,9 @@
     side_columns = after(side_columns, shared)
     side_products = [side_times(side_columns, blocks) for blocks in lower_blocks]
     shared_parts = after(shared_parts, side_products)
-    parent_side = mixed_times(places, shared_parts, lower_middle) - jnp.concatenate(
-        side_products, axis=1
-    )
-
-    global_rows = grid_index * middle_count + jnp.arange(middle_count, dtype=jnp.int32)
-    global_columns = sibling_index * own_columns + jnp.arange(own_columns, dtype=jnp.int32)
-    on_diagonal = global_rows[:, None] == global_columns[None, :]
-    middle_part = jnp.sum(jnp.where(on_diagonal, middle_inverse, 0.0), axis=0) + jnp.sum(
-        middle_panel * first_side, axis=0
-    )
-    lower_rows = lax.dynamic_slice_in_dim(lower_middle, grid_index * middle_count, middle_count, 0)
-    lower_part = jnp.sum(lower_panel * root_side, axis=0) + jnp.sum(
-        lower_rows * parent_side, axis=0
-    )
+    lower_parent, parent_part = mixed_times(places, shared_parts, lower_middle, side_products)
+
+    lower_part = jnp.sum(lower_panel * root_side, axis=0) + parent_part[0]
 
     total = jnp.concatenate([middle_part, lower_part])
     flip = 1
@@ -370,7 +398,7 @@
         flip *= 2
     middle_total = total[:own_columns]
     lower_total = total[own_columns:]
-    return (-first_side, middle_total, -root_side, -parent_side, lower_diagonal + lower_total)
+    return (middle_cross, middle_total, -root_side, lower_parent, lower_diagonal + lower_total)
 
 
 def solution(mesh):

time: 383 us -> 377 us (0.984)
  other arithmetic: 18.4 us -> 13.4 us
    unnamed x146 -> x134, local copies, waits for them, and re-layouts: 30.8 us -> 29.6 us
  transfers between devices with their start and end apart: 42 -> 42, of which waited for: 17 -> 17; matrix products, arithmetic and copies ran while one was open for 5% -> 6% of each run, Pallas kernels for 28% -> 29%
where the time goes in v3:
time: 377 us; the launch traced here: 376 us
  waiting for transfers between devices  145 us (38%)
  Pallas kernels  135 us (36%)
  local copies, waits for them, and re-layouts  39.8 us (11%)
  starting transfers between devices  28.5 us (8%)
  between operations  14.8 us (4%)
  other arithmetic  13.4 us (4%)
    ppermute x41, waiting for transfers between devices, swap(): return lax.ppermute(value, axis, [(i, i ^ flip) for i in range(count)])  144 us
    pallas_call x4, Pallas kernels, root_times(): pl.pallas_call(functools.partial(root_kernel, count), grid_spec=pltpu.Pre...  62.3 us
    pallas_call x3, Pallas kernels, side_times(): pl.pallas_call(functools.partial(side_kernel, len(columns)), grid=(width...  35 us
    pallas_call x2, Pallas kernels, mixed_times(): pl.pallas_call(functools.partial(mixed_kernel, len(left), len(left[0])),...  32.8 us
    unnamed x134, local copies, waits for them, and re-layouts  29.6 us
    ppermute x41, starting transfers between devices, swap(): return lax.ppermute(value, axis, [(i, i ^ flip) for i in range(count)])  28.5 us
    slice x6, local copies, waits for them, and re-layouts, gather_chips(): onward = [held[0][:half], held[1][half:]]  7.66 us
  transfers between devices with their start and end apart: 42, of which 17 were waited for; matrix products, arithmetic and copies ran while one was open for 6% of the time, Pallas kernels for 29%

profile of v3, /device:TPU:0, one launch (start us, length us, event | category | flops | bytes accessed | tf_op | source)
XLA Modules:
  0.0 376.2 jit_solution(10304542588060600052)
XLA Ops:
  8.8 2.9 collective-permute-start.1
  11.7 1.5 collective-permute-start.3
  14.1 2.5 broadcast_multiply_fusion
  16.6 1.8 fusion.3
  18.9 39.4 %collective-permute-done.1.refs_2_.refs_10_ = f32[512,1024]{1,0:T(8,128)} collective-permute-done((f32[512,1024]{1,0:T(8,128)S(1)}, f32[512,1024]{1,0:T(8,128)}, u32[]{:S(2)}, u32[]{:S(2)}) %collective-permute-start.1) | collective-permute-done | bytes 2097184 | tf_op jit(solution)/shard_map/ppermute | solution.py:257
  58.3 2.1 collective-permute-done.3.refs_4_.refs_12_
  60.4 1.3 slice.31
  61.7 1.6 collective-permute-start.5
  63.3 1.3 slice.32
  65.2 37.9 %collective-permute-done.9.refs_2_.refs_10_ = f32[512,1024]{1,0:T(8,128)S(1)} collective-permute-done((f32[512,1024]{1,0:T(8,128)S(1)}, f32[512,1024]{1,0:T(8,128)S(1)}, u32[]{:S(2)}, u32[]{:S(2)}) %collective-permute-start.9) | collective-permute-done | bytes 2097184 | tf_op jit(solution)/shard_map/ppermute | solution.py:257
  103.1 2.1 collective-permute-done.11.refs_4_.refs_12_
  105.4 1.6 collective-permute-start.14
  107.4 20.3 %collective-permute-done.5.refs_6_.refs_14_ = f32[256,1024]{1,0:T(8,128)S(1)} collective-permute-done((f32[256,1024]{1,0:T(8,128)S(1)}, f32[256,1024]{1,0:T(8,128)S(1)}, u32[]{:S(2)}, u32[]{:S(2)}) %collective-permute-start.5) | collective-permute-done | bytes 1048608 | tf_op jit(solution)/shard_map/ppermute | solution.py:257
  127.7 21.0 %collective-permute-done.14.refs_6_.refs_14_ = f32[256,1024]{1,0:T(8,128)S(1)} collective-permute-done((f32[256,1024]{1,0:T(8,128)S(1)}, f32[256,1024]{1,0:T(8,128)S(1)}, u32[]{:S(2)}, u32[]{:S(2)}) %collective-permute-start.14) | collective-permute-done | bytes 1048608 | tf_op jit(solution)/shard_map/ppermute | solution.py:257
  148.7 1.3 collective-permute-done.15.refs_7_.refs_15_
  151.5 1.1 copy-done.9
  157.8 1.7 collective-permute-start.21
  159.6 1.0 copy-done.38
  160.6 1.0 copy-done.41
  162.0 1.2 copy-done.6
  163.2 1.2 copy-done.10
  164.4 1.2 copy-done.14
  165.6 1.2 copy-done.18
  166.9 11.5 %shard_map.110.refs_0_ = f32[256,1024]{1,0:T(8,128)S(1)} custom-call(s32[1]{0:T(128)} %bitcast.index_ref, f32[512,4096]{1,0:T(8,128)} %all-gather.2.cloned.1.call-done.root_ref, f32[512,1024]{1,0:T(8,128)S(1)} %copy-done, f32[512,1024]{1,0:T(8,128)} %collective-permute-done.refs_1_.refs_9_, f32[512,1024]{1,0:T(8,128)} %collective-permute-done.1.refs_2_.refs_10_, ...), custom_call_target="tpu_custom_call" | custom-call | tf_op jit(solution)/shard_map/pallas_call | solution.py:139
  178.3 1.3 collective-permute-start.18
  179.7 1.4 select_reduce_fusion
  181.2 1.2 copy-done.7
  182.4 1.2 copy-done.11
  183.6 1.2 copy-done.15
  184.8 1.2 copy-done.19
  186.1 11.4 %shard_map.111.refs_0_.refs_1_ = f32[256,1024]{1,0:T(8,128)S(1)} custom-call(s32[1]{0:T(128)} %bitcast.index_ref, f32[512,4096]{1,0:T(8,128)} %all-gather.2.cloned.1.call-done.root_ref, f32[512,1024]{1,0:T(8,128)S(1)} %copy-done, f32[512,1024]{1,0:T(8,128)} %collective-permute-done.refs_1_.refs_9_, f32[512,1024]{1,0:T(8,128)} %collective-permute-done.1.refs_2_.refs_10_, ...), custom_call_target="tpu_custom_call" | custom-call | tf_op jit(solution)/shard_map/pallas_call | solution.py:139
  197.5 1.9 multiply_reduce_fusion.1
  199.4 6.3 %collective-permute-done.20.refs_2_.refs_10_ = f32[512,1024]{1,0:T(8,128)} collective-permute-done((f32[512,1024]{1,0:T(8,128)}, f32[512,1024]{1,0:T(8,128)}, u32[]{:S(2)}, u32[]{:S(2)}) %collective-permute-start.20) | collective-permute-done | bytes 2097184 | tf_op jit(solution)/shard_map/ppermute | solution.py:257
  205.8 1.7 shard_map.112
  207.6 1.8 collective-permute-start.23
  209.9 2.5 slice.36
  212.4 1.5 collective-permute-start.27
  213.9 2.3 slice.37
  216.2 1.5 collective-permute-start.28
  217.7 1.1 shard_map.113
  219.7 19.6 %shard_map.114 = f32[512,1024]{1,0:T(8,128)S(1)} custom-call(s32[1]{0:T(128)} %bitcast.index_ref, f32[512,4096]{1,0:T(8,128)} %all-gather.2.cloned.1.call-done.root_ref, f32[512,1024]{1,0:T(8,128)S(1)} %copy-done.2, f32[512,1024]{1,0:T(8,128)} %copy-done.60, f32[512,1024]{1,0:T(8,128)} %copy-done.58, f32[512,1024]{1,0:T(8,128)} %copy-done.61, ...), custom_call_target="tpu_custom_call" | custom-call | tf_op jit(solution)/shard_map/pallas_call | solution.py:139
  242.9 1.0 collective-permute-start.31
  243.9 1.2 shard_map.116
  246.6 1.9 collective-permute-start.35
  249.4 1.0 collective-permute-start.32
  250.4 1.0 copy-done.53
  252.1 5.6 %collective-permute-done.31.refs_2_ = f32[512,256]{1,0:T(8,128)S(1)} collective-permute-done((f32[512,256]{1,0:T(8,128)S(1)}, f32[512,256]{1,0:T(8,128)S(1)}, u32[]{:S(2)}, u32[]{:S(2)}) %collective-permute-start.31) | collective-permute-done | bytes 524320 | tf_op jit(solution)/shard_map/ppermute | solution.py:257
  258.5 1.0 collective-permute-start.36
  259.6 1.2 copy-done.31
  260.8 18.5 %shard_map.117 = f32[512,2048]{1,0:T(8,128)S(1)} custom-call(s32[3]{0:T(128)S(1)} %pad_add_fusion.places_ref, f32[256,1024]{1,0:T(8,128)S(1)} %shard_map.110.refs_0_, f32[256,1024]{1,0:T(8,128)S(1)} %copy-done.4, f32[256,1024]{1,0:T(8,128)} %collective-permute-done.18.refs_1_.refs_2_, f32[256,1024]{1,0:T(8,128)S(1)} %copy-done.31, f32[2048,2048]{1,0:T(8,128)} %refs_6_.1, ...), custom_call_target="tpu_custom_call" | custom-call | tf_op jit(solution)/shard_map/pallas_call | solution.py:234
  279.4 19.8 %shard_map.118 = f32[512,1024]{1,0:T(8,128)S(1)} custom-call(s32[1]{0:T(128)} %bitcast.index_ref, f32[512,4096]{1,0:T(8,128)} %all-gather.2.cloned.1.call-done.root_ref, f32[512,1024]{1,0:T(8,128)} %get-tuple-element.58.refs_0_.refs_8_, f32[512,1024]{1,0:T(8,128)} %collective-permute-done.19.refs_1_.refs_9_, ...), custom_call_target="tpu_custom_call" | custom-call | tf_op jit(solution)/shard_map/pallas_call | solution.py:139
  299.3 1.0 copy-done.26
  300.3 1.0 copy-done.28
  301.4 11.5 %shard_map.119 = f32[256,1024]{1,0:T(8,128)S(1)} custom-call(f32[512,256]{1,0:T(8,128)S(1)} %copy-done.24, f32[512,256]{1,0:T(8,128)S(1)} %copy-done.28, f32[512,256]{1,0:T(8,128)S(1)} %copy-done.26, f32[512,256]{1,0:T(8,128)} %collective-permute-done.32.refs_3_, f32[512,256]{1,0:T(8,128)} %collective-permute-done.33.refs_4_, ...), custom_call_target="tpu_custom_call" | custom-call | tf_op jit(solution)/shard_map/pallas_call | solution.py:164
  314.5 5.9 %fusion.1 = (f32[512,2048]{1,0:T(8,128)}, f32[2048]{0:T(1024)S(1)}) fusion(f32[512,2048]{1,0:T(8,128)S(1)} %shard_map.117, f32[512,1024]{1,0:T(8,128)S(1)} %shard_map.118, f32[512,1024]{1,0:T(8,128)S(1)} %copy-done.22, f32[512,2048]{1,0:T(8,128)} %param.10, f32[512]{0:T(512)S(1)} %broadcast_bitcast_fusion), kind=kLoop, calls=%fused_computation.6 | loop fusion | flops 6289408 | bytes 16787456 | tf_op jit(solution)/shard_map/neg | solution.py:401
  320.4 1.2 copy-done.55
  321.6 11.9 %shard_map.121.refs_5_ = f32[256,1024]{1,0:T(8,128)S(1)} custom-call(f32[512,256]{1,0:T(8,128)S(1)} %copy-done.24, f32[512,256]{1,0:T(8,128)S(1)} %copy-done.29, f32[512,256]{1,0:T(8,128)S(1)} %copy-done.26, f32[512,256]{1,0:T(8,128)} %collective-permute-done.32.refs_3_, f32[512,256]{1,0:T(8,128)} %collective-permute-done.33.refs_4_, ...), custom_call_target="tpu_custom_call" | custom-call | tf_op jit(solution)/shard_map/pallas_call | solution.py:164
  333.6 11.5 %shard_map.120.refs_4_ = f32[256,1024]{1,0:T(8,128)S(1)} custom-call(f32[512,256]{1,0:T(8,128)S(1)} %copy-done.24, f32[512,256]{1,0:T(8,128)S(1)} %copy-done.29, f32[512,256]{1,0:T(8,128)S(1)} %copy-done.26, f32[512,256]{1,0:T(8,128)} %collective-permute-done.32.refs_3_, f32[512,256]{1,0:T(8,128)} %collective-permute-done.33.refs_4_, ...), custom_call_target="tpu_custom_call" | custom-call | tf_op jit(solution)/shard_map/pallas_call | solution.py:164
  345.2 14.3 %shard_map.122 = (f32[256,2048]{1,0:T(8,128)}, f32[1,2048]{1,0:T(1,128)S(1)}) custom-call(s32[3]{0:T(128)S(1)} %pad_add_fusion.places_ref, f32[256,1024]{1,0:T(8,128)S(1)} %add.100.refs_0_, f32[256,1024]{1,0:T(8,128)} %collective-permute-done.37.refs_1_, f32[2048,2048]{1,0:T(8,128)} %refs_6_.1, f32[2048,2048]{1,0:T(8,128)} %refs_6_.1, ...), custom_call_target="tpu_custom_call" | custom-call | tf_op jit(solution)/shard_map/pallas_call | solution.py:234
  359.6 1.2 collective-permute-done.38
  360.8 1.2 collective-permute-start.39
  362.0 2.5 collective-permute-done.39
  364.5 1.4 collective-permute-start.40
  365.9 2.3 collective-permute-done.40
  (194 shorter events, 23.1 us)
Async XLA Ops:
  7.2 154.8 %all-gather.2.cloned.1.call-start = ((), (), s32[]{:S(2)}) async-start(), calls=%async_computation | async-start | bytes 10485760 | tf_op jit(solution)/shard_map/all_gather | solution.py:322
  8.8 49.5 %collective-permute-start.1 = (f32[512,1024]{1,0:T(8,128)S(1)}, f32[512,1024]{1,0:T(8,128)}, u32[]{:S(2)}, u32[]{:S(2)}) collective-permute-start(f32[512,1024]{1,0:T(8,128)S(1)} %copy-done), channel_id=1, source_target_pairs={{0,2},{1,3},{2,0},{3,1},{4,6},{5,7},{6,4},{7,5},{8,10},{9,11},{10,... | collective-permute-start | bytes 6291464 | tf_op jit(solution)/shard_map/ppermute | solution.py:257
  11.7 48.7 %collective-permute-start.3 = (f32[512,1024]{1,0:T(8,128)S(1)}, f32[512,1024]{1,0:T(8,128)}, u32[]{:S(2)}, u32[]{:S(2)}) collective-permute-start(f32[512,1024]{1,0:T(8,128)S(1)} %copy-done), channel_id=1, source_target_pairs={{0,4},{1,5},{2,6},{3,7},{4,0},{5,1},{6,2},{7,3},{8,12},{9,13},{10,... | collective-permute-start | bytes 6291464 | tf_op jit(solution)/shard_map/ppermute | solution.py:257
  13.2 47.1 %collective-permute-start = (f32[512,1024]{1,0:T(8,128)S(1)}, f32[512,1024]{1,0:T(8,128)}, u32[]{:S(2)}, u32[]{:S(2)}) collective-permute-start(f32[512,1024]{1,0:T(8,128)S(1)} %copy-done), channel_id=1, source_target_pairs={{0,1},{1,0},{2,3},{3,2},{4,5},{5,4},{6,7},{7,6},{8,9},{9,8},{10,11... | collective-permute-start | bytes 6291464 | tf_op jit(solution)/shard_map/ppermute | solution.py:257
  18.3 46.3 %copy-start.1 = (f32[512,1024]{1,0:T(8,128)}, f32[512,1024]{1,0:T(8,128)S(1)}, u32[]{:S(2)}) copy-start(f32[512,1024]{1,0:T(8,128)S(1)} %get-tuple-element.109.refs_0_.refs_8_) | copy-start | bytes 6291460
  18.4 84.7 %collective-permute-start.9 = (f32[512,1024]{1,0:T(8,128)S(1)}, f32[512,1024]{1,0:T(8,128)S(1)}, u32[]{:S(2)}, u32[]{:S(2)}) collective-permute-start(f32[512,1024]{1,0:T(8,128)S(1)} %get-tuple-element.109.refs_0_.refs_8_), channel_id=1, source_target_pairs={{0,2},{1,3},{2,0},{3,1},{4,6},{5,7},{6,4},{7,5},{8,10},{9,11},{10,... | collective-permute-start | bytes 6291464 | tf_op jit(solution)/shard_map/ppermute | solution.py:257
  18.9 86.3 %collective-permute-start.11 = (f32[512,1024]{1,0:T(8,128)S(1)}, f32[512,1024]{1,0:T(8,128)S(1)}, u32[]{:S(2)}, u32[]{:S(2)}) collective-permute-start(f32[512,1024]{1,0:T(8,128)S(1)} %get-tuple-element.109.refs_0_.refs_8_), channel_id=1, source_target_pairs={{0,4},{1,5},{2,6},{3,7},{4,0},{5,1},{6,2},{7,3},{8,12},{9,13},{10,... | collective-permute-start | bytes 6291464 | tf_op jit(solution)/shard_map/ppermute | solution.py:257
  58.3 46.9 %collective-permute-start.13 = (f32[512,1024]{1,0:T(8,128)S(1)}, f32[512,1024]{1,0:T(8,128)S(1)}, u32[]{:S(2)}, u32[]{:S(2)}) collective-permute-start(f32[512,1024]{1,0:T(8,128)S(1)} %get-tuple-element.109.refs_0_.refs_8_), channel_id=1, source_target_pairs={{0,1},{1,0},{2,3},{3,2},{4,5},{5,4},{6,7},{7,6},{8,9},{9,8},{10,11... | collective-permute-start | bytes 6291464 | tf_op jit(solution)/shard_map/ppermute | solution.py:257
  61.7 66.0 %collective-permute-start.5 = (f32[256,1024]{1,0:T(8,128)S(1)}, f32[256,1024]{1,0:T(8,128)S(1)}, u32[]{:S(2)}, u32[]{:S(2)}) collective-permute-start(f32[256,1024]{1,0:T(8,128)S(1)} %slice.31), channel_id=1, source_target_pairs={{0,4},{1,5},{2,6},{3,7},{4,0},{5,1},{6,2},{7,3},{8,12},{9,13},{10,... | collective-permute-start | bytes 3145736 | tf_op jit(solution)/shard_map/ppermute | solution.py:257
  64.6 63.0 %collective-permute-start.6 = (f32[256,1024]{1,0:T(8,128)S(1)}, f32[256,1024]{1,0:T(8,128)S(1)}, u32[]{:S(2)}, u32[]{:S(2)}) collective-permute-start(f32[256,1024]{1,0:T(8,128)S(1)} %slice.32), channel_id=1, source_target_pairs={{0,2},{1,3},{2,0},{3,1},{4,6},{5,7},{6,4},{7,5},{8,10},{9,11},{10,... | collective-permute-start | bytes 3145736 | tf_op jit(solution)/shard_map/ppermute | solution.py:257
  105.2 54.4 %copy-start.60 = (f32[512,1024]{1,0:T(8,128)}, f32[512,1024]{1,0:T(8,128)S(1)}, u32[]{:S(2)}) copy-start(f32[512,1024]{1,0:T(8,128)S(1)} %collective-permute-done.13.refs_1_.refs_9_) | copy-start | bytes 6291460
  105.2 45.8 %collective-permute-start.10 = (f32[512,1024]{1,0:T(8,128)S(1)}, f32[512,1024]{1,0:T(8,128)S(1)}, u32[]{:S(2)}, u32[]{:S(2)}) collective-permute-start(f32[512,1024]{1,0:T(8,128)S(1)} %collective-permute-done.9.refs_2_.refs_10_), channel_id=1, source_target_pairs={{0,1},{1,0},{2,3},{3,2},{4,5},{5,4},{6,7},{7,6},{8,9},{9,8},{10,11... | collective-permute-start | bytes 6291464 | tf_op jit(solution)/shard_map/ppermute | solution.py:257
  105.4 43.3 %collective-permute-start.14 = (f32[256,1024]{1,0:T(8,128)S(1)}, f32[256,1024]{1,0:T(8,128)S(1)}, u32[]{:S(2)}, u32[]{:S(2)}) collective-permute-start(f32[256,1024]{1,0:T(8,128)S(1)} %slice.34), channel_id=1, source_target_pairs={{0,4},{1,5},{2,6},{3,7},{4,0},{5,1},{6,2},{7,3},{8,12},{9,13},{10,... | collective-permute-start | bytes 3145736 | tf_op jit(solution)/shard_map/ppermute | solution.py:257
  107.1 45.5 %collective-permute-start.12 = (f32[512,1024]{1,0:T(8,128)S(1)}, f32[512,1024]{1,0:T(8,128)S(1)}, u32[]{:S(2)}, u32[]{:S(2)}) collective-permute-start(f32[512,1024]{1,0:T(8,128)S(1)} %collective-permute-done.11.refs_4_.refs_12_), channel_id=1, source_target_pairs={{0,1},{1,0},{2,3},{3,2},{4,5},{5,4},{6,7},{7,6},{8,9},{9,8},{10,11... | collective-permute-start | bytes 6291464 | tf_op jit(solution)/shard_map/ppermute | solution.py:257
  127.7 22.3 %collective-permute-start.15 = (f32[256,1024]{1,0:T(8,128)S(1)}, f32[256,1024]{1,0:T(8,128)S(1)}, u32[]{:S(2)}, u32[]{:S(2)}) collective-permute-start(f32[256,1024]{1,0:T(8,128)S(1)} %slice.35), channel_id=1, source_target_pairs={{0,2},{1,3},{2,0},{3,1},{4,6},{5,7},{6,4},{7,5},{8,10},{9,11},{10,... | collective-permute-start | bytes 3145736 | tf_op jit(solution)/shard_map/ppermute | solution.py:257
  127.7 29.7 %collective-permute-start.2 = (f32[512,1024]{1,0:T(8,128)}, f32[512,1024]{1,0:T(8,128)S(1)}, u32[]{:S(2)}, u32[]{:S(2)}) collective-permute-start(f32[512,1024]{1,0:T(8,128)} %collective-permute-done.1.refs_2_.refs_10_), channel_id=1, source_target_pairs={{0,1},{1,0},{2,3},{3,2},{4,5},{5,4},{6,7},{7,6},{8,9},{9,8},{10,11... | collective-permute-start | bytes 6291464 | tf_op jit(solution)/shard_map/ppermute | solution.py:257
  148.7 8.7 %collective-permute-start.4 = (f32[512,1024]{1,0:T(8,128)}, f32[512,1024]{1,0:T(8,128)S(1)}, u32[]{:S(2)}, u32[]{:S(2)}) collective-permute-start(f32[512,1024]{1,0:T(8,128)} %collective-permute-done.3.refs_4_.refs_12_), channel_id=1, source_target_pairs={{0,1},{1,0},{2,3},{3,2},{4,5},{5,4},{6,7},{7,6},{8,9},{9,8},{10,11... | collective-permute-start | bytes 6291464 | tf_op jit(solution)/shard_map/ppermute | solution.py:257
  150.0 4.3 %collective-permute-start.7 = (f32[256,1024]{1,0:T(8,128)S(1)}, f32[256,1024]{1,0:T(8,128)S(1)}, u32[]{:S(2)}, u32[]{:S(2)}) collective-permute-start(f32[256,1024]{1,0:T(8,128)S(1)} %collective-permute-done.5.refs_6_.refs_14_), channel_id=1, source_target_pairs={{0,1},{1,0},{2,3},{3,2},{4,5},{5,4},{6,7},{7,6},{8,9},{9,8},{10,11... | collective-permute-start | bytes 3145736 | tf_op jit(solution)/shard_map/ppermute | solution.py:257
  151.0 5.4 %collective-permute-start.8 = (f32[256,1024]{1,0:T(8,128)S(1)}, f32[256,1024]{1,0:T(8,128)S(1)}, u32[]{:S(2)}, u32[]{:S(2)}) collective-permute-start(f32[256,1024]{1,0:T(8,128)S(1)} %collective-permute-done.6.refs_7_.refs_15_), channel_id=1, source_target_pairs={{0,1},{1,0},{2,3},{3,2},{4,5},{5,4},{6,7},{7,6},{8,9},{9,8},{10,11... | collective-permute-start | bytes 3145736 | tf_op jit(solution)/shard_map/ppermute | solution.py:257
  152.6 6.9 %collective-permute-start.16 = (f32[256,1024]{1,0:T(8,128)S(1)}, f32[256,1024]{1,0:T(8,128)S(1)}, u32[]{:S(2)}, u32[]{:S(2)}) collective-permute-start(f32[256,1024]{1,0:T(8,128)S(1)} %collective-permute-done.14.refs_6_.refs_14_), channel_id=1, source_target_pairs={{0,1},{1,0},{2,3},{3,2},{4,5},{5,4},{6,7},{7,6},{8,9},{9,8},{10,11... | collective-permute-start | bytes 3145736 | tf_op jit(solution)/shard_map/ppermute | solution.py:257
  155.3 5.3 %collective-permute-start.17 = (f32[256,1024]{1,0:T(8,128)S(1)}, f32[256,1024]{1,0:T(8,128)S(1)}, u32[]{:S(2)}, u32[]{:S(2)}) collective-permute-start(f32[256,1024]{1,0:T(8,128)S(1)} %collective-permute-done.15.refs_7_.refs_15_), channel_id=1, source_target_pairs={{0,1},{1,0},{2,3},{3,2},{4,5},{5,4},{6,7},{7,6},{8,9},{9,8},{10,11... | collective-permute-start | bytes 3145736 | tf_op jit(solution)/shard_map/ppermute | solution.py:257
  157.4 48.3 %collective-permute-start.20 = (f32[512,1024]{1,0:T(8,128)}, f32[512,1024]{1,0:T(8,128)}, u32[]{:S(2)}, u32[]{:S(2)}) collective-permute-start(f32[512,1024]{1,0:T(8,128)} %get-tuple-element.58.refs_0_.refs_8_), channel_id=1, source_target_pairs={{0,2},{1,3},{2,0},{3,1},{4,6},{5,7},{6,4},{7,5},{8,10},{9,11},{10,... | collective-permute-start | bytes 6291464 | tf_op jit(solution)/shard_map/ppermute | solution.py:257
  157.8 48.0 %collective-permute-start.21 = (f32[512,1024]{1,0:T(8,128)}, f32[512,1024]{1,0:T(8,128)}, u32[]{:S(2)}, u32[]{:S(2)}) collective-permute-start(f32[512,1024]{1,0:T(8,128)} %get-tuple-element.58.refs_0_.refs_8_), channel_id=1, source_target_pairs={{0,4},{1,5},{2,6},{3,7},{4,0},{5,1},{6,2},{7,3},{8,12},{9,13},{10,... | collective-permute-start | bytes 6291464 | tf_op jit(solution)/shard_map/ppermute | solution.py:257
  159.6 46.3 %collective-permute-start.19 = (f32[512,1024]{1,0:T(8,128)}, f32[512,1024]{1,0:T(8,128)}, u32[]{:S(2)}, u32[]{:S(2)}) collective-permute-start(f32[512,1024]{1,0:T(8,128)} %get-tuple-element.58.refs_0_.refs_8_), channel_id=1, source_target_pairs={{0,1},{1,0},{2,3},{3,2},{4,5},{5,4},{6,7},{7,6},{8,9},{9,8},{10,11... | collective-permute-start | bytes 6291464 | tf_op jit(solution)/shard_map/ppermute | solution.py:257
  178.3 27.5 %collective-permute-start.18 = (f32[256,1024]{1,0:T(8,128)S(1)}, f32[256,1024]{1,0:T(8,128)}, u32[]{:S(2)}, u32[]{:S(2)}) collective-permute-start(f32[256,1024]{1,0:T(8,128)S(1)} %shard_map.110.refs_0_), channel_id=1, source_target_pairs={{0,8},{8,0},{16,24},{24,16},{1,9},{9,1},{17,25},{25,17},{2,10},{10... | collective-permute-start | bytes 3145736 | tf_op jit(solution)/shard_map/ppermute | solution.py:257
  197.5 41.8 %copy-start.3 = (f32[256,1024]{1,0:T(8,128)}, f32[256,1024]{1,0:T(8,128)S(1)}, u32[]{:S(2)}) copy-start(f32[256,1024]{1,0:T(8,128)S(1)} %shard_map.111.refs_0_.refs_1_) | copy-start | bytes 3145732
  207.5 8.7 %collective-permute-start.22 = (f32[1024,256]{1,0:T(8,128)S(1)}, f32[1024,256]{1,0:T(8,128)S(1)}, u32[]{:S(2)}, u32[]{:S(2)}) collective-permute-start(f32[1024,256]{1,0:T(8,128)S(1)} %get-tuple-element.66), channel_id=1, source_target_pairs={{0,1},{1,0},{2,3},{3,2},{4,5},{5,4},{6,7},{7,6},{8,9},{9,8},{10,11... | collective-permute-start | bytes 3145736 | tf_op jit(solution)/shard_map/ppermute | solution.py:257
  207.6 31.8 %collective-permute-start.23 = (f32[256,1024]{1,0:T(8,128)S(1)}, f32[256,1024]{1,0:T(8,128)S(1)}, u32[]{:S(2)}, u32[]{:S(2)}) collective-permute-start(f32[256,1024]{1,0:T(8,128)S(1)} %shard_map.111.refs_0_.refs_1_), channel_id=1, source_target_pairs={{0,8},{8,0},{16,24},{24,16},{1,9},{9,1},{17,25},{25,17},{2,10},{10... | collective-permute-start | bytes 3145736 | tf_op jit(solution)/shard_map/ppermute | solution.py:257
  209.4 36.6 %collective-permute-start.25 = (f32[512,1024]{1,0:T(8,128)}, f32[512,1024]{1,0:T(8,128)S(1)}, u32[]{:S(2)}, u32[]{:S(2)}) collective-permute-start(f32[512,1024]{1,0:T(8,128)} %collective-permute-done.20.refs_2_.refs_10_), channel_id=1, source_target_pairs={{0,1},{1,0},{2,3},{3,2},{4,5},{5,4},{6,7},{7,6},{8,9},{9,8},{10,11... | collective-permute-start | bytes 6291464 | tf_op jit(solution)/shard_map/ppermute | solution.py:257
  209.5 37.0 %collective-permute-start.26 = (f32[512,1024]{1,0:T(8,128)}, f32[512,1024]{1,0:T(8,128)S(1)}, u32[]{:S(2)}, u32[]{:S(2)}) collective-permute-start(f32[512,1024]{1,0:T(8,128)} %collective-permute-done.21.refs_4_.refs_12_), channel_id=1, source_target_pairs={{0,1},{1,0},{2,3},{3,2},{4,5},{5,4},{6,7},{7,6},{8,9},{9,8},{10,11... | collective-permute-start | bytes 6291464 | tf_op jit(solution)/shard_map/ppermute | solution.py:257
  212.4 27.9 %collective-permute-start.27 = (f32[256,1024]{1,0:T(8,128)}, f32[256,1024]{1,0:T(8,128)S(1)}, u32[]{:S(2)}, u32[]{:S(2)}) collective-permute-start(f32[256,1024]{1,0:T(8,128)} %slice.36), channel_id=1, source_target_pairs={{0,4},{1,5},{2,6},{3,7},{4,0},{5,1},{6,2},{7,3},{8,12},{9,13},{10,... | collective-permute-start | bytes 3145736 | tf_op jit(solution)/shard_map/ppermute | solution.py:257
  216.2 25.2 %collective-permute-start.28 = (f32[256,1024]{1,0:T(8,128)}, f32[256,1024]{1,0:T(8,128)S(1)}, u32[]{:S(2)}, u32[]{:S(2)}) collective-permute-start(f32[256,1024]{1,0:T(8,128)} %slice.37), channel_id=1, source_target_pairs={{0,2},{1,3},{2,0},{3,1},{4,6},{5,7},{6,4},{7,5},{8,10},{9,11},{10,... | collective-permute-start | bytes 3145736 | tf_op jit(solution)/shard_map/ppermute | solution.py:257
  240.2 19.4 %copy-start.4 = (f32[256,1024]{1,0:T(8,128)S(1)}, f32[256,1024]{1,0:T(8,128)}, u32[]{:S(2)}) copy-start(f32[256,1024]{1,0:T(8,128)} %copy-done.3) | copy-start | bytes 3145732
  240.2 2.7 collective-permute-start.24
  240.3 17.4 %copy-start.44 = (f32[256,1024]{1,0:T(8,128)}, f32[256,1024]{1,0:T(8,128)S(1)}, u32[]{:S(2)}) copy-start(f32[256,1024]{1,0:T(8,128)S(1)} %collective-permute-done.27.refs_6_.refs_14_) | copy-start | bytes 3145732
  240.3 8.2 %collective-permute-start.29 = (f32[256,1024]{1,0:T(8,128)S(1)}, f32[256,1024]{1,0:T(8,128)S(1)}, u32[]{:S(2)}, u32[]{:S(2)}) collective-permute-start(f32[256,1024]{1,0:T(8,128)S(1)} %collective-permute-done.27.refs_6_.refs_14_), channel_id=1, source_target_pairs={{0,1},{1,0},{2,3},{3,2},{4,5},{5,4},{6,7},{7,6},{8,9},{9,8},{10,11... | collective-permute-start | bytes 3145736 | tf_op jit(solution)/shard_map/ppermute | solution.py:257
  241.4 9.0 %collective-permute-start.30 = (f32[256,1024]{1,0:T(8,128)S(1)}, f32[256,1024]{1,0:T(8,128)S(1)}, u32[]{:S(2)}, u32[]{:S(2)}) collective-permute-start(f32[256,1024]{1,0:T(8,128)S(1)} %collective-permute-done.28.refs_7_.refs_15_), channel_id=1, source_target_pairs={{0,1},{1,0},{2,3},{3,2},{4,5},{5,4},{6,7},{7,6},{8,9},{9,8},{10,11... | collective-permute-start | bytes 3145736 | tf_op jit(solution)/shard_map/ppermute | solution.py:257
  242.9 14.8 %collective-permute-start.31 = (f32[512,256]{1,0:T(8,128)S(1)}, f32[512,256]{1,0:T(8,128)S(1)}, u32[]{:S(2)}, u32[]{:S(2)}) collective-permute-start(f32[512,256]{1,0:T(8,128)S(1)} %get-tuple-element.68), channel_id=1, source_target_pairs={{0,2},{1,3},{2,0},{3,1},{4,6},{5,7},{6,4},{7,5},{8,10},{9,11},{10,... | collective-permute-start | bytes 1572872 | tf_op jit(solution)/shard_map/ppermute | solution.py:257
  245.9 12.5 %copy-start.63 = (f32[512,1024]{1,0:T(8,128)}, f32[512,1024]{1,0:T(8,128)S(1)}, u32[]{:S(2)}) copy-start(f32[512,1024]{1,0:T(8,128)S(1)} %collective-permute-done.25.refs_3_.refs_11_) | copy-start | bytes 6291460
  245.9 53.2 %collective-permute-start.33 = (f32[512,256]{1,0:T(8,128)}, f32[512,256]{1,0:T(8,128)}, u32[]{:S(2)}, u32[]{:S(2)}) collective-permute-start(f32[512,256]{1,0:T(8,128)} %get-tuple-element.69), channel_id=1, source_target_pairs={{0,4},{1,5},{2,6},{3,7},{4,0},{5,1},{6,2},{7,3},{8,12},{9,13},{10,... | collective-permute-start | bytes 1572872 | tf_op jit(solution)/shard_map/ppermute | solution.py:257
  246.6 11.9 %copy-start.64 = (f32[512,1024]{1,0:T(8,128)}, f32[512,1024]{1,0:T(8,128)S(1)}, u32[]{:S(2)}) copy-start(f32[512,1024]{1,0:T(8,128)S(1)} %collective-permute-done.26.refs_5_.refs_13_) | copy-start | bytes 6291460
  246.6 52.6 %collective-permute-start.35 = (f32[512,256]{1,0:T(8,128)}, f32[512,256]{1,0:T(8,128)}, u32[]{:S(2)}, u32[]{:S(2)}) collective-permute-start(f32[512,256]{1,0:T(8,128)} %get-tuple-element.70), channel_id=1, source_target_pairs={{0,6},{1,7},{2,4},{3,5},{4,2},{5,3},{6,0},{7,1},{8,14},{9,15},{10,... | collective-permute-start | bytes 1572872 | tf_op jit(solution)/shard_map/ppermute | solution.py:257
  249.4 49.8 %collective-permute-start.32 = (f32[512,256]{1,0:T(8,128)}, f32[512,256]{1,0:T(8,128)}, u32[]{:S(2)}, u32[]{:S(2)}) collective-permute-start(f32[512,256]{1,0:T(8,128)} %get-tuple-element.77), channel_id=1, source_target_pairs={{0,2},{1,3},{2,0},{3,1},{4,6},{5,7},{6,4},{7,5},{8,10},{9,11},{10,... | collective-permute-start | bytes 1572872 | tf_op jit(solution)/shard_map/ppermute | solution.py:257
  251.5 47.7 %collective-permute-start.34 = (f32[512,256]{1,0:T(8,128)}, f32[512,256]{1,0:T(8,128)}, u32[]{:S(2)}, u32[]{:S(2)}) collective-permute-start(f32[512,256]{1,0:T(8,128)} %get-tuple-element.78), channel_id=1, source_target_pairs={{0,4},{1,5},{2,6},{3,7},{4,0},{5,1},{6,2},{7,3},{8,12},{9,13},{10,... | collective-permute-start | bytes 1572872 | tf_op jit(solution)/shard_map/ppermute | solution.py:257
  258.5 40.7 %collective-permute-start.36 = (f32[512,256]{1,0:T(8,128)}, f32[512,256]{1,0:T(8,128)}, u32[]{:S(2)}, u32[]{:S(2)}) collective-permute-start(f32[512,256]{1,0:T(8,128)} %get-tuple-element.79), channel_id=1, source_target_pairs={{0,6},{1,7},{2,4},{3,5},{4,2},{5,3},{6,0},{7,1},{8,14},{9,15},{10,... | collective-permute-start | bytes 1572872 | tf_op jit(solution)/shard_map/ppermute | solution.py:257
  260.8 18.5 %copy-start.45 = (f32[256,1024]{1,0:T(8,128)S(1)}, f32[256,1024]{1,0:T(8,128)}, u32[]{:S(2)}) copy-start(f32[256,1024]{1,0:T(8,128)} %copy-done.44) | copy-start | bytes 3145732
  260.8 18.5 %copy-start.48 = (f32[256,1024]{1,0:T(8,128)S(1)}, f32[256,1024]{1,0:T(8,128)}, u32[]{:S(2)}) copy-start(f32[256,1024]{1,0:T(8,128)} %copy-done.47) | copy-start | bytes 3145732
  260.8 18.5 %copy-start.51 = (f32[256,1024]{1,0:T(8,128)S(1)}, f32[256,1024]{1,0:T(8,128)}, u32[]{:S(2)}) copy-start(f32[256,1024]{1,0:T(8,128)} %copy-done.50) | copy-start | bytes 3145732
  260.8 18.5 %copy-start.54 = (f32[256,1024]{1,0:T(8,128)S(1)}, f32[256,1024]{1,0:T(8,128)}, u32[]{:S(2)}) copy-start(f32[256,1024]{1,0:T(8,128)} %copy-done.53) | copy-start | bytes 3145732
  279.3 19.9 %copy-start.8 = (f32[256,1024]{1,0:T(8,128)S(1)}, f32[256,1024]{1,0:T(8,128)}, u32[]{:S(2)}) copy-start(f32[256,1024]{1,0:T(8,128)} %copy-done.5) | copy-start | bytes 3145732
  279.3 19.9 %copy-start.12 = (f32[256,1024]{1,0:T(8,128)S(1)}, f32[256,1024]{1,0:T(8,128)}, u32[]{:S(2)}) copy-start(f32[256,1024]{1,0:T(8,128)} %copy-done.9) | copy-start | bytes 3145732
  279.3 19.9 %copy-start.16 = (f32[256,1024]{1,0:T(8,128)S(1)}, f32[256,1024]{1,0:T(8,128)}, u32[]{:S(2)}) copy-start(f32[256,1024]{1,0:T(8,128)} %copy-done.13) | copy-start | bytes 3145732
  279.3 19.9 %copy-start.20 = (f32[256,1024]{1,0:T(8,128)S(1)}, f32[256,1024]{1,0:T(8,128)}, u32[]{:S(2)}) copy-start(f32[256,1024]{1,0:T(8,128)} %copy-done.17) | copy-start | bytes 3145732
  279.4 19.9 %copy-start.24 = (f32[512,256]{1,0:T(8,128)S(1)}, f32[512,256]{1,0:T(8,128)}, u32[]{:S(2)}) copy-start(f32[512,256]{1,0:T(8,128)} %copy-done.23) | copy-start | bytes 1572868
  279.4 33.5 %copy-start.65 = (f32[256,1024]{1,0:T(8,128)S(1)}, f32[256,1024]{1,0:T(8,128)}, u32[]{:S(2)}) copy-start(f32[256,1024]{1,0:T(8,128)} %param.8) | copy-start | bytes 3145732
  313.1 32.1 %collective-permute-start.37 = (f32[256,1024]{1,0:T(8,128)S(1)}, f32[256,1024]{1,0:T(8,128)}, u32[]{:S(2)}, u32[]{:S(2)}) collective-permute-start(f32[256,1024]{1,0:T(8,128)S(1)} %add.100.refs_0_), channel_id=1, source_target_pairs={{0,8},{8,0},{16,24},{24,16},{1,9},{9,1},{17,25},{25,17},{2,10},{10... | collective-permute-start | bytes 3145736 | tf_op jit(solution)/shard_map/ppermute | solution.py:257
  321.6 11.9 %copy-start.34 = (f32[256,1024]{1,0:T(8,128)S(1)}, f32[256,1024]{1,0:T(8,128)}, u32[]{:S(2)}) copy-start(f32[256,1024]{1,0:T(8,128)} %copy-done.32) | copy-start | bytes 3145732
  321.6 12.0 %copy-start.37 = (f32[256,1024]{1,0:T(8,128)S(1)}, f32[256,1024]{1,0:T(8,128)}, u32[]{:S(2)}) copy-start(f32[256,1024]{1,0:T(8,128)} %copy-done.35) | copy-start | bytes 3145732
  321.6 12.0 %copy-start.40 = (f32[256,1024]{1,0:T(8,128)S(1)}, f32[256,1024]{1,0:T(8,128)}, u32[]{:S(2)}) copy-start(f32[256,1024]{1,0:T(8,128)} %copy-done.38) | copy-start | bytes 3145732
  321.6 12.0 %copy-start.43 = (f32[256,1024]{1,0:T(8,128)S(1)}, f32[256,1024]{1,0:T(8,128)}, u32[]{:S(2)}) copy-start(f32[256,1024]{1,0:T(8,128)} %copy-done.41) | copy-start | bytes 3145732
  345.2 23.6 %copy-start.66 = (f32[2048]{0:T(1024)S(1)}, f32[2048]{0:T(1024)}, u32[]{:S(2)}) copy-start(f32[2048]{0:T(1024)} %param.13) | copy-start | bytes 24580
  359.5 1.2 collective-permute-start.38
  360.8 3.7 collective-permute-start.39
  364.5 3.7 collective-permute-start.40
  (45 other events, 139.1 us)
Sparse Core Ops, SparseCore 0:
  9.6 152.3 all-gather.1
